TPU v7x, 32 devices: a whole 2x2x4 slice. The times are simulated.
32 devices in a mesh: groups: 2 (over y), wide: 4 (over z), narrow: 2 (over x), inner: 2 (over core).
Axes of the slice: x: 2, y: 2, z: 4, core: 2. Of those that a mesh axis runs over, the one named last changes fastest.
Arguments:
- land_cover: int32 [192, 512], P(('groups', 'wide'), ('narrow', 'inner')), parts along dimension 0, may hold values from 0 to 15
- prune_mask: int32 [2, 192, 512], P(None, ('groups', 'wide'), ('narrow', 'inner')), parts along dimension 1, may hold values 0 or 1
- class_resistance: float32 [16], replicated, may hold values from 1 to 100
- source_cells: int32 [256], P('groups'), parts along dimension 0, may hold values from 0 to 49151
- ground_cells: int32 [256], P('groups'), parts along dimension 0, may hold values from 0 to 49151
- warm_start: float32 [128, 192, 512], P(None, ('groups', 'wide'), ('narrow', 'inner')), parts along dimension 1, may hold values from -24 to 24
Outputs:
- potentials: float32 [128, 192, 512], P(None, ('groups', 'wide'), ('narrow', 'inner')), parts along dimension 1
- residual: float32 [128, 192, 512], P(None, ('groups', 'wide'), ('narrow', 'inner')), parts along dimension 1
There are 2 independent parts, one for each index of `groups`. A program takes and returns all parts, laid end to end along the dimension named above; an argument that names none is the same for every part. Nothing has to cross between parts.
All inputs are finite; a program needn't handle non-finite values. No bound on the sum of `prune_mask` on one device may be relied on, other than what follows from the above.
Results may differ from a plain program's by a relative error of at most 0.0025.
Values sent between devices are 32-bit elements; how exact they have to be, the bound alone decides.
A program may use at most 64 MiB of HBM per device.

v0:
```python
import jax
import jax.numpy as jnp
from jax import lax
from jax.sharding import PartitionSpec as P

ITERS = 2


LEAK = 0.1


def passed_along(value, axis, steps):
    count = lax.axis_size(axis)
    leading, last = (max(0, -steps), min(count, count - steps))
    return lax.ppermute(value, axis, [(source, source + steps) for source in range(leading, last)])


def with_halo(block, sides, width):
    for axis, dim in sides:
        count = lax.axis_size(axis)
        forward = [(i, i + 1) for i in range(count - 1)]
        backward = [(target, source) for source, target in forward]
        low = lax.ppermute(
            lax.slice_in_dim(block, block.shape[dim] - width, None, axis=dim), axis, forward
        )
        high = lax.ppermute(lax.slice_in_dim(block, 0, width, axis=dim), axis, backward)
        block = jnp.concatenate([low, block, high], axis=dim)
    return block


def resist(cover, table):
    classes = jnp.arange(table.shape[0], dtype=jnp.int32)
    hit = cover[None] == classes[:, None, None]
    return jnp.sum(jnp.where(hit, table[:, None, None], jnp.float32(0.0)), 0)


def gram(left, right):
    count = left.shape[0]
    return jnp.dot(
        left.reshape(count, -1), right.reshape(count, -1).T, precision=lax.Precision.HIGHEST
    )


def symm(matrix):
    return 0.5 * (matrix + matrix.T)


def spd_solve(matrix, rhs):
    factor = jnp.linalg.cholesky(matrix)
    return jax.scipy.linalg.cho_solve((factor, True), rhs)


def combine(coeffs, field):
    count = field.shape[0]
    out = jnp.dot(coeffs.T, field.reshape(count, -1), precision=lax.Precision.HIGHEST)
    return out.reshape(field.shape)


def per_device(land_cover, prune_mask, class_resistance, source_cells, ground_cells, warm_start):
    tile_rows, tile_cols = land_cover.shape
    total_rows = tile_rows * lax.axis_size("wide")
    total_cols = tile_cols * lax.axis_size(("narrow", "inner"))
    row_start = lax.axis_index("wide") * tile_rows
    col_start = lax.axis_index(("narrow", "inner")) * tile_cols
    next_row = passed_along(land_cover[:1], "wide", -1)
    next_col = passed_along(land_cover[:, :1], ("narrow", "inner"), -1)
    res_here = resist(land_cover, class_resistance)
    res_below = jnp.concatenate([res_here[1:], resist(next_row, class_resistance)], 0)
    res_right = jnp.concatenate([res_here[:, 1:], resist(next_col, class_resistance)], 1)
    col_glob = col_start + lax.broadcasted_iota(jnp.int32, (tile_rows, tile_cols), 1)
    row_glob = row_start + lax.broadcasted_iota(jnp.int32, (tile_rows, tile_cols), 0)
    keep_right = (1 - prune_mask[0]).astype(jnp.float32) * (col_glob < total_cols - 1).astype(
        jnp.float32
    )
    keep_down = (1 - prune_mask[1]).astype(jnp.float32) * (row_glob < total_rows - 1).astype(
        jnp.float32
    )
    right_own = keep_right * 2.0 / (res_here + res_right)
    down_own = keep_down * 2.0 / (res_here + res_below)
    above_edges = passed_along(down_own[-1:], "wide", 1)
    left_edges = passed_along(right_own[:, -1:], ("narrow", "inner"), 1)
    down_up = jnp.concatenate([above_edges, down_own[:-1]], 0)
    right_left = jnp.concatenate([left_edges, right_own[:, :-1]], 1)

    def operate(field):
        padded = with_halo(field, (("wide", 1), (("narrow", "inner"), 2)), 1)
        center = padded[:, 1:-1, 1:-1]
        total = LEAK * center
        total = total + right_own * (center - padded[:, 1:-1, 2:])
        total = total + right_left * (center - padded[:, 1:-1, :-2])
        total = total + down_own * (center - padded[:, 2:, 1:-1])
        total = total + down_up * (center - padded[:, :-2, 1:-1])
        return total

    flat = (
        (row_start + lax.broadcasted_iota(jnp.int32, (tile_rows, tile_cols), 0)) * total_cols
        + col_start
        + lax.broadcasted_iota(jnp.int32, (tile_rows, tile_cols), 1)
    )
    currents = (flat[None] == source_cells[:, None, None]).astype(jnp.float32) - (
        flat[None] == ground_cells[:, None, None]
    ).astype(jnp.float32)
    potentials = warm_start
    residual = currents - operate(potentials)
    direction = residual
    norm_now = symm(lax.psum(gram(residual, residual), ("wide", "narrow", "inner")))
    for step in range(ITERS):
        image = operate(direction)
        last = step + 1 == ITERS
        curv = symm(lax.psum(gram(direction, image), ("wide", "narrow", "inner")))
        alpha = spd_solve(curv, norm_now)
        potentials = potentials + combine(alpha, direction)
        residual = residual - combine(alpha, image)
        if not last:
            norm_next = symm(lax.psum(gram(residual, residual), ("wide", "narrow", "inner")))
        if not last:
            beta = spd_solve(norm_now, norm_next)
            direction = residual + combine(beta, direction)
            norm_now = norm_next
    return (potentials, residual)


def solution(mesh):
    in_specs = (
        P(("groups", "wide"), ("narrow", "inner")),
        P(None, ("groups", "wide"), ("narrow", "inner")),
        P(),
        P("groups"),
        P("groups"),
        P(None, ("groups", "wide"), ("narrow", "inner")),
    )
    out_specs = (
        P(None, ("groups", "wide"), ("narrow", "inner")),
        P(None, ("groups", "wide"), ("narrow", "inner")),
    )
    return jax.shard_map(
        per_device, mesh=mesh, in_specs=in_specs, out_specs=out_specs, check_vma=False
    )
```

profile of v0, /device:TPU:0, one launch (start us, length us, event | category | flops | bytes accessed | tf_op | source)
XLA Modules:
  0.0 441.7 jit_solution(2945057724743199498)
XLA Ops:
  7.2 0.7 slice.139
  7.9 1.3 collective-permute-start.6
  9.2 1.4 collective-permute-start
  10.7 1.9 copy.76
  12.6 1.3 collective-permute-start.2
  13.9 6.2 %collective-permute-start.1 = (f32[128,1,128]{0,2,1:T(8,128)S(1)}, f32[128,1,128]{0,2,1:T(8,128)S(1)}, u32[]{:S(2)}, u32[]{:S(2)}) collective-permute-start(f32[128,1,128]{0,2,1:T(8,128)S(1)} %get-tuple-element.23), channel_id=1, source_target_pairs={{0,4},{4,8},{8,12},{1,5},{5,9},{9,13},{2,6},{6,10},{10,14},{3,7},{... | collective-permute-start | bytes 196616 | tf_op jit(solution)/shard_map/ppermute | solution.py:23
  21.0 3.9 collective-permute-start.7
  25.0 2.5 collective-permute-start.4
  27.5 0.7 collective-permute-done.4
  28.4 1.3 collective-permute-start.3
  29.7 4.6 %collective-permute-start.5 = (f32[128,26,1]{0,2,1:T(1,128)S(1)}, f32[128,26,1]{0,2,1:T(1,128)S(1)}, u32[]{:S(2)}, u32[]{:S(2)}) collective-permute-start(f32[128,26,1]{0,2,1:T(1,128)S(1)} %get-tuple-element.17), channel_id=1, source_target_pairs={{0,1},{1,2},{2,3},{4,5},{5,6},{6,7},{8,9},{9,10},{10,11},{12,13},{... | collective-permute-start | bytes 39944 | tf_op jit(solution)/shard_map/ppermute | solution.py:23
  34.4 0.8 collective-permute-done.5
  35.1 3.6 fusion.27
  38.7 1.3 collective-permute-start.9
  40.0 4.5 %collective-permute-start.8 = (f32[128,1,128]{0,2,1:T(8,128)S(1)}, f32[128,1,128]{0,2,1:T(8,128)S(1)}, u32[]{:S(2)}, u32[]{:S(2)}) collective-permute-start(f32[128,1,128]{0,2,1:T(8,128)S(1)} %get-tuple-element.21), channel_id=1, source_target_pairs={{0,4},{4,8},{8,12},{1,5},{5,9},{9,13},{2,6},{6,10},{10,14},{3,7},{... | collective-permute-start | bytes 196616 | tf_op jit(solution)/shard_map/ppermute | solution.py:23
  44.6 0.3 collective-permute-done.9
  44.9 1.6 collective-permute-done.8
  46.5 1.3 collective-permute-start.10
  47.8 3.7 collective-permute-start.11
  51.5 3.3 convolution_bitcast_fusion.5
  54.8 4.9 %convolution_bitcast_fusion.6 = f32[128,128]{1,0:T(8,128)} fusion(f32[128,24,128]{0,2,1:T(8,128)S(1)} %fusion.27, f32[128,1,128]{0,2,1:T(8,128)S(1)} %collective-permute-done.8, f32[128,1,128]{0,2,1:T(8,128)S(1)} %collective-permute-done.9, f32[128,26,1]{0,2,1:T(1,128)S(1)} %collective-permute-done.11, f32[128,26,1]{0,2,1:T(1,128)S(1)} %collective-permute-done.10, ...), kind=kOutput, calls=%fused_computation.82 | convolution fusion | flops 612237312 | bytes 1845248 | tf_op jit(solution)/shard_map/dot_general | solution.py:39
  59.7 0.3 all-reduce.5.cloned.1.call-start
  60.1 90.3 %all-reduce.9.cloned.1.call-done = (f32[128,128]{1,0:T(8,128)}, f32[128,128]{1,0:T(8,128)}) async-done(((f32[128,128]{1,0:T(8,128)}, f32[128,128]{1,0:T(8,128)}), (f32[128,128]{1,0:T(8,128)}, f32[128,128]{1,0:T(8,128)})) %all-reduce.9.cloned.1.call-update) | async-done | bytes 131088 | tf_op jit(solution)/shard_map/psum | solution.py:106
  150.3 0.9 copy.94
  151.3 0.9 copy.90
  152.2 0.9 fusion.70
  153.2 11.7 %cholesky.59 = f32[128,128]{1,0:T(8,128)S(1)} custom-call(f32[128,128]{1,0:T(8,128)S(1)} %fusion.74), custom_call_target="Cholesky" | custom-call | tf_op jit(solution)/shard_map/jit(cholesky)/cholesky | solution.py:49
  165.0 0.6 compare_reduce_fusion.2
  165.6 0.7 fusion.57
  166.3 9.8 %custom-call.9 = f32[1,128,128]{1,2,0:T(8,128)S(1)} custom-call(f32[1,128,128]{2,1,0:T(8,128)S(1)} %fusion.57), custom_call_target="InvertDiagBlocksLowerTriangular" | custom-call | tf_op jit(solution)/shard_map/jit(_cho_solve)/triangular_solve | solution.py:50
  176.2 0.3 fusion.72
  176.7 11.7 %cholesky.70 = f32[128,128]{1,0:T(8,128)S(1)} custom-call(f32[128,128]{1,0:T(8,128)S(1)} %fusion.69), custom_call_target="Cholesky" | custom-call | tf_op jit(solution)/shard_map/jit(cholesky)/cholesky | solution.py:49
  188.5 0.6 compare_reduce_fusion.1
  189.1 3.2 fusion.51
  192.3 1.1 copy-done
  193.4 3.3 convolution_bitcast_fusion.3
  196.8 0.6 fusion.58
  197.3 9.8 %custom-call.10 = f32[1,128,128]{1,2,0:T(8,128)S(1)} custom-call(f32[1,128,128]{2,1,0:T(8,128)S(1)} %fusion.58), custom_call_target="InvertDiagBlocksLowerTriangular" | custom-call | tf_op jit(solution)/shard_map/jit(_cho_solve)/triangular_solve | solution.py:50
  207.2 76.0 %all-reduce.5.cloned.1.call-done = f32[128,128]{1,0:T(8,128)} async-done(((f32[128,128]{1,0:T(8,128)}), f32[128,128]{1,0:T(8,128)}) %all-reduce.5.cloned.1.call-update) | async-done | bytes 65552 | tf_op jit(solution)/shard_map/psum | solution.py:115
  283.2 0.9 copy.100
  284.1 1.1 fusion.67
  285.5 2.8 fusion.48
  288.3 1.3 collective-permute-start.13
  289.6 6.6 %collective-permute-start.12 = (f32[128,1,128]{0,2,1:T(8,128)S(1)}, f32[128,1,128]{0,2,1:T(8,128)S(1)}, u32[]{:S(2)}, u32[]{:S(2)}) collective-permute-start(f32[128,1,128]{0,2,1:T(8,128)S(1)} %get-tuple-element.19), channel_id=1, source_target_pairs={{0,4},{4,8},{8,12},{1,5},{5,9},{9,13},{2,6},{6,10},{10,14},{3,7},{... | collective-permute-start | bytes 196616 | tf_op jit(solution)/shard_map/ppermute | solution.py:23
  296.2 0.3 collective-permute-done.13
  296.5 1.6 collective-permute-done.12
  298.1 1.3 collective-permute-start.14
  299.4 3.3 collective-permute-start.15
  302.7 0.6 collective-permute-done.15
  303.4 4.9 %convolution_bitcast_fusion.1 = f32[128,128]{1,0:T(8,128)} fusion(f32[128,24,128]{0,2,1:T(8,128)S(1)} %fusion.48, f32[128,1,128]{0,2,1:T(8,128)S(1)} %collective-permute-done.12, f32[128,1,128]{0,2,1:T(8,128)S(1)} %collective-permute-done.13, f32[128,26,1]{0,2,1:T(1,128)S(1)} %collective-permute-done.15, f32[128,26,1]{0,2,1:T(1,128)S(1)} %collective-permute-done.14, ...), kind=kOutput, calls=%fused_computation.77 | convolution fusion | flops 612237312 | bytes 1845248 | tf_op jit(solution)/shard_map/dot_general | solution.py:39
  308.4 86.9 %all-reduce.7.cloned.1.call-done = f32[128,128]{1,0:T(8,128)} async-done(((f32[128,128]{1,0:T(8,128)}), f32[128,128]{1,0:T(8,128)}) %all-reduce.7.cloned.1.call-update) | async-done | bytes 65552 | tf_op jit(solution)/shard_map/psum | solution.py:110
  395.3 0.9 copy.103
  396.2 0.9 fusion.64
  397.2 11.7 %cholesky.81 = f32[128,128]{1,0:T(8,128)S(1)} custom-call(f32[128,128]{1,0:T(8,128)S(1)} %fusion.63), custom_call_target="Cholesky" | custom-call | tf_op jit(solution)/shard_map/jit(cholesky)/cholesky | solution.py:49
  408.9 0.6 compare_reduce_fusion
  409.6 0.7 fusion.59
  410.2 9.8 %custom-call.11 = f32[1,128,128]{1,2,0:T(8,128)S(1)} custom-call(f32[1,128,128]{2,1,0:T(8,128)S(1)} %fusion.59), custom_call_target="InvertDiagBlocksLowerTriangular" | custom-call | tf_op jit(solution)/shard_map/jit(_cho_solve)/triangular_solve | solution.py:50
  420.1 0.3 fusion.61
  420.4 0.3 convolution_bitcast_fusion
  420.7 1.7 fusion.39
  422.4 1.8 fusion.47
  424.3 2.1 copy.108
  426.5 5.5 %fusion.54 = f32[128,24,128]{0,2,1:T(8,128)} fusion(f32[128,24,128]{0,2,1:T(8,128)S(1)} %copy-done.1, f32[128,128,1]{0,1,2:T(8,128)S(1)} %convolution_bitcast_fusion, f32[128,24,128]{0,2,1:T(8,128)S(1)} %fusion.48, f32[128,1,128]{0,2,1:T(8,128)S(1)} %copy-done.8, f32[128,1,128]{0,2,1:T(8,128)S(1)} %copy-done.6, f32[128,26,1]{0,2,1:T(1,128)S(1)} %copy-done.22, ...), kind=kOutput, calls=%fused_computation.75 | convolution fusion | flops 612630528 | bytes 4990976 | tf_op jit(solution)/shard_map/dot_general | solution.py:55
  431.9 3.0 copy.109
  (94 shorter events, 2.2 us)
Async XLA Ops:
  7.2 143.2 %all-reduce.9.cloned.1.call-start = ((), (), s32[]{:S(2)}) async-start(), calls=%async_computation.2 | async-start | bytes 262144 | tf_op jit(solution)/shard_map/psum | solution.py:106
  7.9 12.9 %collective-permute-start.6 = (s32[1,128]{1,0:T(1,128)S(1)}, s32[1,128]{1,0:T(1,128)S(1)}, u32[]{:S(2)}, u32[]{:S(2)}) collective-permute-start(s32[1,128]{1,0:T(1,128)S(1)} %slice.139), channel_id=1, source_target_pairs={{4,0},{8,4},{12,8},{5,1},{9,5},{13,9},{6,2},{10,6},{14,10},{7,3},{... | collective-permute-start | bytes 1544 | tf_op jit(solution)/shard_map/ppermute | solution.py:15
  9.2 10.9 %copy-start.15 = (s32[24,128]{1,0:T(8,128)S(1)}, s32[24,128]{1,0:T(8,128)}, u32[]{:S(2)}) copy-start(s32[24,128]{1,0:T(8,128)} %param.9) | copy-start | bytes 36868
  9.2 10.9 %copy-start.16 = (f32[16]{0:T(128)S(1)}, f32[16]{0:T(128)}, u32[]{:S(2)}) copy-start(f32[16]{0:T(128)} %param.11) | copy-start | bytes 196
  9.2 11.7 %copy-start.4 = (s32[2,24,128]{2,1,0:T(8,128)S(1)}, s32[2,24,128]{2,1,0:T(8,128)}, u32[]{:S(2)}) copy-start(s32[2,24,128]{2,1,0:T(8,128)} %param.10) | copy-start | bytes 73732
  9.2 11.2 %collective-permute-start = (s32[24,1]{1,0:T(8,128)}, s32[24,1]{1,0:T(8,128)S(1)}, u32[]{:S(2)}, u32[]{:S(2)}) collective-permute-start(s32[24,1]{1,0:T(8,128)} %bitcast.153), channel_id=1, source_target_pairs={{1,0},{2,1},{3,2},{5,4},{6,5},{7,6},{9,8},{10,9},{11,10},{13,12},{... | collective-permute-start | bytes 296 | tf_op jit(solution)/shard_map/ppermute | solution.py:15
  12.5 22.6 %copy-start.17 = (s32[128]{0:T(128)S(1)}, s32[128]{0:T(128)}, u32[]{:S(2)}) copy-start(s32[128]{0:T(128)} %param.13) | copy-start | bytes 1540
  12.6 22.6 %copy-start.18 = (s32[128]{0:T(128)S(1)}, s32[128]{0:T(128)}, u32[]{:S(2)}) copy-start(s32[128]{0:T(128)} %param.12) | copy-start | bytes 1540
  12.6 15.8 %collective-permute-start.2 = (f32[128,1,128]{0,2,1:T(8,128)S(1)}, f32[128,1,128]{0,2,1:T(8,128)S(1)}, u32[]{:S(2)}, u32[]{:S(2)}) collective-permute-start(f32[128,1,128]{0,2,1:T(8,128)S(1)} %get-tuple-element.22), channel_id=1, source_target_pairs={{4,0},{8,4},{12,8},{5,1},{9,5},{13,9},{6,2},{10,6},{14,10},{7,3},{... | collective-permute-start | bytes 196616 | tf_op jit(solution)/shard_map/ppermute | solution.py:26
  13.9 14.5 %collective-permute-start.1 = (f32[128,1,128]{0,2,1:T(8,128)S(1)}, f32[128,1,128]{0,2,1:T(8,128)S(1)}, u32[]{:S(2)}, u32[]{:S(2)}) collective-permute-start(f32[128,1,128]{0,2,1:T(8,128)S(1)} %get-tuple-element.23), channel_id=1, source_target_pairs={{0,4},{4,8},{8,12},{1,5},{5,9},{9,13},{2,6},{6,10},{10,14},{3,7},{... | collective-permute-start | bytes 196616 | tf_op jit(solution)/shard_map/ppermute | solution.py:23
  21.0 13.4 %collective-permute-start.7 = (f32[1,128]{1,0:T(1,128)S(1)}, f32[1,128]{1,0:T(1,128)S(1)}, u32[]{:S(2)}, u32[]{:S(2)}) collective-permute-start(f32[1,128]{1,0:T(1,128)S(1)} %slice.166), channel_id=1, source_target_pairs={{0,4},{4,8},{8,12},{1,5},{5,9},{9,13},{2,6},{6,10},{10,14},{3,7},{... | collective-permute-start | bytes 1544 | tf_op jit(solution)/shard_map/ppermute | solution.py:15
  25.0 3.3 collective-permute-start.4
  27.5 275.8 %copy-start.9 = (f32[24,128]{1,0:T(8,128)}, f32[24,128]{1,0:T(8,128)S(1)}, u32[]{:S(2)}) copy-start(f32[24,128]{1,0:T(8,128)S(1)} %get-tuple-element.25) | copy-start | bytes 36868
  28.3 275.0 %copy-start.13 = (f32[24,128]{1,0:T(8,128)}, f32[24,128]{1,0:T(8,128)S(1)}, u32[]{:S(2)}) copy-start(f32[24,128]{1,0:T(8,128)S(1)} %pad_maximum_fusion.33) | copy-start | bytes 36868
  28.4 6.0 %collective-permute-start.3 = (f32[128,26,1]{0,2,1:T(1,128)S(1)}, f32[128,26,1]{0,2,1:T(1,128)S(1)}, u32[]{:S(2)}, u32[]{:S(2)}) collective-permute-start(f32[128,26,1]{0,2,1:T(1,128)S(1)} %get-tuple-element.16), channel_id=1, source_target_pairs={{1,0},{2,1},{3,2},{5,4},{6,5},{7,6},{9,8},{10,9},{11,10},{13,12},{... | collective-permute-start | bytes 39944 | tf_op jit(solution)/shard_map/ppermute | solution.py:26
  29.7 5.5 %collective-permute-start.5 = (f32[128,26,1]{0,2,1:T(1,128)S(1)}, f32[128,26,1]{0,2,1:T(1,128)S(1)}, u32[]{:S(2)}, u32[]{:S(2)}) collective-permute-start(f32[128,26,1]{0,2,1:T(1,128)S(1)} %get-tuple-element.17), channel_id=1, source_target_pairs={{0,1},{1,2},{2,3},{4,5},{5,6},{6,7},{8,9},{9,10},{10,11},{12,13},{... | collective-permute-start | bytes 39944 | tf_op jit(solution)/shard_map/ppermute | solution.py:23
  34.3 269.0 %copy-start.11 = (f32[24,128]{1,0:T(8,128)}, f32[24,128]{1,0:T(8,128)S(1)}, u32[]{:S(2)}) copy-start(f32[24,128]{1,0:T(8,128)S(1)} %pad_maximum_fusion.34) | copy-start | bytes 36868
  38.7 6.2 %collective-permute-start.9 = (f32[128,1,128]{0,2,1:T(8,128)S(1)}, f32[128,1,128]{0,2,1:T(8,128)S(1)}, u32[]{:S(2)}, u32[]{:S(2)}) collective-permute-start(f32[128,1,128]{0,2,1:T(8,128)S(1)} %get-tuple-element.20), channel_id=1, source_target_pairs={{4,0},{8,4},{12,8},{5,1},{9,5},{13,9},{6,2},{10,6},{14,10},{7,3},{... | collective-permute-start | bytes 196616 | tf_op jit(solution)/shard_map/ppermute | solution.py:26
  40.0 6.4 %collective-permute-start.8 = (f32[128,1,128]{0,2,1:T(8,128)S(1)}, f32[128,1,128]{0,2,1:T(8,128)S(1)}, u32[]{:S(2)}, u32[]{:S(2)}) collective-permute-start(f32[128,1,128]{0,2,1:T(8,128)S(1)} %get-tuple-element.21), channel_id=1, source_target_pairs={{0,4},{4,8},{8,12},{1,5},{5,9},{9,13},{2,6},{6,10},{10,14},{3,7},{... | collective-permute-start | bytes 196616 | tf_op jit(solution)/shard_map/ppermute | solution.py:23
  46.5 8.3 %collective-permute-start.10 = (f32[128,26,1]{0,2,1:T(1,128)S(1)}, f32[128,26,1]{0,2,1:T(1,128)S(1)}, u32[]{:S(2)}, u32[]{:S(2)}) collective-permute-start(f32[128,26,1]{0,2,1:T(1,128)S(1)} %get-tuple-element.14), channel_id=1, source_target_pairs={{1,0},{2,1},{3,2},{5,4},{6,5},{7,6},{9,8},{10,9},{11,10},{13,12},{... | collective-permute-start | bytes 39944 | tf_op jit(solution)/shard_map/ppermute | solution.py:26
  47.8 7.0 %collective-permute-start.11 = (f32[128,26,1]{0,2,1:T(1,128)S(1)}, f32[128,26,1]{0,2,1:T(1,128)S(1)}, u32[]{:S(2)}, u32[]{:S(2)}) collective-permute-start(f32[128,26,1]{0,2,1:T(1,128)S(1)} %get-tuple-element.15), channel_id=1, source_target_pairs={{0,1},{1,2},{2,3},{4,5},{5,6},{6,7},{8,9},{9,10},{10,11},{12,13},{... | collective-permute-start | bytes 39944 | tf_op jit(solution)/shard_map/ppermute | solution.py:23
  59.7 223.5 %all-reduce.5.cloned.1.call-start = ((), (), s32[]{:S(2)}) async-start(), calls=%async_computation | async-start | bytes 131072 | tf_op jit(solution)/shard_map/psum | solution.py:115
  192.3 1.1 copy-start
  196.7 198.6 %all-reduce.7.cloned.1.call-start = ((), (), s32[]{:S(2)}) async-start(), calls=%async_computation.1 | async-start | bytes 131072 | tf_op jit(solution)/shard_map/psum | solution.py:110
  288.3 8.2 %collective-permute-start.13 = (f32[128,1,128]{0,2,1:T(8,128)S(1)}, f32[128,1,128]{0,2,1:T(8,128)S(1)}, u32[]{:S(2)}, u32[]{:S(2)}) collective-permute-start(f32[128,1,128]{0,2,1:T(8,128)S(1)} %get-tuple-element.18), channel_id=1, source_target_pairs={{4,0},{8,4},{12,8},{5,1},{9,5},{13,9},{6,2},{10,6},{14,10},{7,3},{... | collective-permute-start | bytes 196616 | tf_op jit(solution)/shard_map/ppermute | solution.py:26
  289.6 8.5 %collective-permute-start.12 = (f32[128,1,128]{0,2,1:T(8,128)S(1)}, f32[128,1,128]{0,2,1:T(8,128)S(1)}, u32[]{:S(2)}, u32[]{:S(2)}) collective-permute-start(f32[128,1,128]{0,2,1:T(8,128)S(1)} %get-tuple-element.19), channel_id=1, source_target_pairs={{0,4},{4,8},{8,12},{1,5},{5,9},{9,13},{2,6},{6,10},{10,14},{3,7},{... | collective-permute-start | bytes 196616 | tf_op jit(solution)/shard_map/ppermute | solution.py:23
  296.5 6.9 %copy-start.5 = (f32[128,1,128]{0,2,1:T(8,128)}, f32[128,1,128]{0,2,1:T(8,128)S(1)}, u32[]{:S(2)}) copy-start(f32[128,1,128]{0,2,1:T(8,128)S(1)} %collective-permute-done.13) | copy-start | bytes 196612
  298.0 5.3 %copy-start.7 = (f32[128,1,128]{0,2,1:T(8,128)}, f32[128,1,128]{0,2,1:T(8,128)S(1)}, u32[]{:S(2)}) copy-start(f32[128,1,128]{0,2,1:T(8,128)S(1)} %collective-permute-done.12) | copy-start | bytes 196612
  298.1 4.7 %collective-permute-start.14 = (f32[128,26,1]{0,2,1:T(1,128)S(1)}, f32[128,26,1]{0,2,1:T(1,128)S(1)}, u32[]{:S(2)}, u32[]{:S(2)}) collective-permute-start(f32[128,26,1]{0,2,1:T(1,128)S(1)} %get-tuple-element.12), channel_id=1, source_target_pairs={{1,0},{2,1},{3,2},{5,4},{6,5},{7,6},{9,8},{10,9},{11,10},{13,12},{... | collective-permute-start | bytes 39944 | tf_op jit(solution)/shard_map/ppermute | solution.py:26
  299.4 120.7 %copy-start.3 = (f32[128,128]{1,0:T(8,128)S(1)}, f32[128,128]{1,0:T(8,128)}, u32[]{:S(2)}) copy-start(f32[128,128]{1,0:T(8,128)} %all-reduce.5.cloned.1.call-done) | copy-start | bytes 196612
  299.4 4.0 collective-permute-start.15
  302.7 5.6 %copy-start.19 = (f32[128,26,1]{0,2,1:T(1,128)}, f32[128,26,1]{0,2,1:T(1,128)S(1)}, u32[]{:S(2)}) copy-start(f32[128,26,1]{0,2,1:T(1,128)S(1)} %collective-permute-done.14) | copy-start | bytes 39940
  303.4 4.9 %copy-start.21 = (f32[128,26,1]{0,2,1:T(1,128)}, f32[128,26,1]{0,2,1:T(1,128)S(1)}, u32[]{:S(2)}) copy-start(f32[128,26,1]{0,2,1:T(1,128)S(1)} %collective-permute-done.15) | copy-start | bytes 39940
  420.7 1.7 copy-start.2
  424.3 2.1 copy-start.1
  424.3 2.1 copy-start.6
  424.3 2.1 copy-start.8
  424.3 2.1 copy-start.10
  424.3 2.1 copy-start.12
  424.3 2.1 copy-start.14
  424.3 2.1 copy-start.20
  424.3 2.1 copy-start.22
Sparse Core Ops, SparseCore 0:
  59.8 90.4 all-reduce.8
  196.8 86.3 all-reduce.4
  308.5 86.7 all-reduce.6
where the time goes:
time: 450 us; the launch traced here: 442 us
  waiting for transfers between devices  259 us (58%)
  other arithmetic  74.6 us (17%)
  starting transfers between devices  46.2 us (10%)
  matrix products  33.8 us (8%)
  between operations  14.7 us (3%)
  local copies, waits for them, and re-layouts  13.2 us (3%)
    psum x2, waiting for transfers between devices, per_device(): lax.psum(gram(residual, residual), ('wide', 'narrow', 'inner'))  166 us
    psum x1, waiting for transfers between devices, per_device(): curv = symm(lax.psum(gram(direction, image), ('wide', 'narrow', 'inner')))  86.9 us
    another operation x9, other arithmetic, spd_solve(): factor = jnp.linalg.cholesky(matrix)  37.2 us
    another operation x6, other arithmetic, spd_solve(): return jax.scipy.linalg.cho_solve((factor, True), rhs)  31.3 us
    ppermute x6, starting transfers between devices, with_halo(): lax.ppermute(lax.slice_in_dim(block, block.shape[dim] - width, None, axis...  29 us
    dot_general x4, matrix products, gram(): jnp.dot(left.reshape(count, -1), right.reshape(count, -1).T, precision=la...  16.4 us
    dot_general x5, matrix products, combine(): jnp.dot(coeffs.T, field.reshape(count, -1), precision=lax.Precision.HIGHEST)  15 us
    ppermute x4, starting transfers between devices, passed_along(): lax.ppermute(value, axis, [(source, source + steps) for source in range(l...  9.09 us
  transfers between devices with their start and end apart: 19, of which 10 were waited for; matrix products, arithmetic and copies ran while one was open for 4% of the time, Pallas kernels for 0%

commit v1 on v0

v1 whole, which is shorter than its diff:
```python
import functools
import jax
import jax.numpy as jnp
from jax import lax
from jax.experimental import pallas as pl
from jax.experimental.pallas import tpu as pltpu
from jax.sharding import PartitionSpec as P

LEAK = 0.1
MESH = pl.DeviceIdType.MESH
F32 = jnp.float32
GROUP = 16
BLOCK = 16
NT = (((1,), (1,)), ((), ()))
NN = (((1,), (0,)), ((), ()))


def split(x):
    hi = x.astype(jnp.bfloat16)
    return hi, (x - hi.astype(F32)).astype(jnp.bfloat16)


def dot3(a, b, dims):
    (ah, al), (bh, bl) = a, b
    mm = functools.partial(lax.dot_general, dimension_numbers=dims, preferred_element_type=F32)
    return mm(ah, bh) + (mm(ah, bl) + mm(al, bh))


def stages_of(count):
    out, stride = [], 1
    while count > 1:
        g = min(GROUP, count)
        assert count % g == 0
        out.append((g, stride))
        stride *= g
        count //= g
    return out


def krylov_kernel(sizes, pieces, cover_ref, prune_ref, table_ref, src_ref, gnd_ref, x_ref,
                  r0_ref, w1_ref, w2_ref, gram_ref,
                  fx, f0, f1, packs, lefts, rights, edge, edge_up, edge_down, side, side_left, side_right,
                  cond, sg, hsend, hrecv, isend, irecv, gsend, grecv, *bufs):
    wide_n, narrow_n, inner_n = sizes
    pairs = fx.shape[1]
    rows, cols = cover_ref.shape
    cells_n = narrow_n * inner_n
    stages = stages_of(wide_n * cells_n)
    w = lax.axis_index("wide")
    c = lax.axis_index("narrow") * inner_n + lax.axis_index("inner")
    rank = w * cells_n + c

    def dev(rk):
        return {"wide": rk // cells_n, "narrow": (rk % cells_n) // inner_n, "inner": rk % inner_n}

    has_up, has_down = w > 0, w < wide_n - 1
    has_left, has_right = c > 0, c < cells_n - 1
    sides = ((has_up, rank - cells_n), (has_down, rank + cells_n), (has_left, rank - 1), (has_right, rank + 1))

    def peer(stage, o):
        g, stride = stages[stage]
        digit = (rank // stride) % g
        other = (digit + o) % g
        return other, rank + (other - digit) * stride

    barrier = pltpu.get_barrier_semaphore()
    expect = 0
    for s, (g, _) in enumerate(stages):
        for o in range(1, g):
            pl.semaphore_signal(barrier, inc=1, device_id=dev(peer(s, o)[1]), device_id_type=MESH)
            expect += 1
    near = 0
    if len(stages) > 1:
        for has, rk in sides:
            near = near + has.astype(jnp.int32)

            @pl.when(has)
            def _(rk=rk):
                pl.semaphore_signal(barrier, inc=1, device_id=dev(rk), device_id_type=MESH)

    lane = lax.broadcasted_iota(jnp.int32, (pairs, cols), 1)
    half = pairs // 2
    lane_h = lax.broadcasted_iota(jnp.int32, (half, cols), 1)

    cover = cover_ref[...]
    res = jnp.zeros((rows, cols), F32)
    for k in range(table_ref.shape[0]):
        res = jnp.where(cover == k, table_ref[k], res)
    keep_r = (1 - prune_ref[0]).astype(F32)
    keep_d = (1 - prune_ref[1]).astype(F32)
    side[0] = res
    side[1] = keep_r
    edge[...] = jnp.concatenate([res[:1], res[rows - 1:], keep_d[rows - 1:], res[: 5]], 0)

    zero_row = jnp.zeros((pairs, cols), F32)
    for has, bufs0 in ((has_up, tuple(f.at[0] for f in (fx, f0, f1))),
                       (has_down, tuple(f.at[rows + 1] for f in (fx, f0, f1))),
                       (has_left, tuple(lefts.at[e] for e in range(3))),
                       (has_right, tuple(rights.at[e] for e in range(3)))):
        @pl.when(jnp.logical_not(has))
        def _(bufs0=bufs0):
            for b in bufs0:
                b[...] = zero_row

    for has, ref in ((has_up, edge_up), (has_down, edge_down), (has_left, side_left), (has_right, side_right)):
        @pl.when(jnp.logical_not(has))
        def _(ref=ref):
            ref[...] = jnp.ones(ref.shape, F32)

    packs[0] = zero_row

    def load_row(r, carry):
        v = x_ref[pl.ds(r, pairs, stride=rows), :]
        fx[r + 1] = v
        rolled = pltpu.roll(v, 2 * r, 1)
        packs[0] = jnp.where((lane == 2 * r) | (lane == (2 * r + cols - 1) % cols), rolled, packs[0])
        return carry

    lax.fori_loop(0, rows, load_row, 0)
    pl.semaphore_wait(barrier, expect + near)

    def halo(e):
        field = (fx, f0, f1)[e]
        return (
            (field.at[1], field.at[rows + 1], 0),
            (field.at[rows], field.at[0], 1),
            (packs.at[e], rights.at[e], 2),
            (packs.at[e], lefts.at[e], 3),
        )

    def copies(items, ssem, rsem):
        out = []
        for (src, dst, k), (has, rk) in zip(items, sides):
            out.append((has, pltpu.make_async_remote_copy(
                src_ref=src, dst_ref=dst, send_sem=ssem.at[k], recv_sem=rsem.at[k],
                device_id=dev(rk), device_id_type=MESH)))
        return out

    def start(cs):
        for has, cp in cs:
            @pl.when(has)
            def _(cp=cp):
                cp.start()

    def wait(cs):
        order = (1, 0, 3, 2)
        for k, (has, cp) in enumerate(cs):
            @pl.when(has)
            def _(cp=cp):
                cp.wait_send()

            @pl.when(cs[order[k]][0])
            def _(cp=cp):
                cp.wait_recv()

    info = copies(((edge, edge_down, 0), (edge, edge_up, 1), (side, side_right, 2), (side, side_left, 3)), isend, irecv)
    start(info)
    ex = [copies(halo(e), hsend.at[e], hrecv.at[e]) for e in range(3)]
    start(ex[0])

    src_t = jnp.broadcast_to(src_ref[...].astype(F32), (cols, pairs)).T
    gnd_t = jnp.broadcast_to(gnd_ref[...].astype(F32), (cols, pairs)).T
    sg[0] = src_t
    sg[1] = gnd_t

    wait(info)
    lane_r = lax.broadcasted_iota(jnp.int32, (rows, cols), 1)
    row_r = lax.broadcasted_iota(jnp.int32, (rows, cols), 0)
    right_res = jnp.where(lane_r == cols - 1, pltpu.roll(side_right[0], cols - 1, 1), pltpu.roll(res, cols - 1, 1))
    left_res = jnp.where(lane_r == 0, pltpu.roll(side_left[0], 1, 1), pltpu.roll(res, 1, 1))
    left_keep = jnp.where(lane_r == 0, pltpu.roll(side_left[1], 1, 1), pltpu.roll(keep_r, 1, 1))
    down_res = jnp.where(row_r == rows - 1, edge_down[0:1, :], pltpu.roll(res, rows - 1, 0))
    up_res = jnp.where(row_r == 0, edge_up[1:2, :], pltpu.roll(res, 1, 0))
    up_keep = jnp.where(row_r == 0, edge_up[2:3, :], pltpu.roll(keep_d, 1, 0))
    at_right = (lane_r == cols - 1) & jnp.logical_not(has_right)
    at_left = (lane_r == 0) & jnp.logical_not(has_left)
    at_down = (row_r == rows - 1) & jnp.logical_not(has_down)
    at_up = (row_r == 0) & jnp.logical_not(has_up)
    cond[0] = jnp.where(at_right, 0.0, keep_r * 2.0 / (res + right_res))
    cond[1] = jnp.where(at_left, 0.0, left_keep * 2.0 / (res + left_res))
    cond[2] = jnp.where(at_down, 0.0, keep_d * 2.0 / (res + down_res))
    cond[3] = jnp.where(at_up, 0.0, up_keep * 2.0 / (res + up_res))

    def stencil(e, finish):
        field = (fx, f0, f1)[e]
        even = (lane % 2) == 0
        lefts[e] = jnp.where(even, rights[e], pltpu.roll(lefts[e], 2, 1))
        if e < 2:
            packs[e + 1] = zero_row

        def body(r, carry):
            cr, cl, cd, cu = (cond[k, pl.ds(r, 1), :] for k in range(4))
            for h in range(2):
                hs = pl.ds(h * half, half)
                v = field[r + 1, hs, :]
                edges = pltpu.roll(lefts[e, hs, :], (2 * cols - 2 * r - 1) % cols, 1)
                xr = jnp.where(lane_h == cols - 1, edges, pltpu.roll(v, cols - 1, 1))
                xl = jnp.where(lane_h == 0, edges, pltpu.roll(v, 1, 1))
                lap = cr * (v - xr) + cl * (v - xl) + cd * (v - field[r + 2, hs, :]) + cu * (v - field[r, hs, :])
                out = finish(r, hs, v, lap)
                if e < 2:
                    rolled = pltpu.roll(out, 2 * r, 1)
                    packs[e + 1, hs, :] = jnp.where(
                        (lane_h == 2 * r) | (lane_h == (2 * r + cols - 1) % cols), rolled, packs[e + 1, hs, :])
            return carry

        lax.fori_loop(0, rows, body, 0)

    total_cols = cols * cells_n
    col_f = (lax.broadcasted_iota(jnp.int32, (1, cols), 1) + c * cols)

    def first(r, hs, v, lap):
        flat = (col_f + (w * rows + r) * total_cols).astype(F32)
        cur = (sg[0, hs, :] == flat).astype(F32) - (sg[1, hs, :] == flat).astype(F32)
        out = cur - (LEAK * v + lap)
        f0[r + 1, hs, :] = out
        r0_ref[r, hs, :] = out
        return out

    def second(r, hs, v, lap):
        f1[r + 1, hs, :] = lap
        w1_ref[r, hs, :] = lap
        return lap

    def third(r, hs, v, lap):
        w2_ref[r, hs, :] = lap
        return lap

    def two_rows(ref, i, off):
        return split(jnp.concatenate([ref[2 * i + off], ref[2 * i + 1 + off]], 1))

    nst = len(stages)
    gl = bufs[:nst + 1]
    rb = bufs[nst + 1:]
    offs = [sum(pieces[:k]) for k in range(len(pieces))]

    def reduce_start(s, k):
        g, _ = stages[s]
        n = pieces[k] // g
        for o in range(1, g):
            other, rk = peer(s, o)
            pltpu.make_async_remote_copy(
                src_ref=gl[s].at[pl.ds(pl.multiple_of(offs[k] + other * n, 8), n)],
                dst_ref=rb[s * len(pieces) + k].at[o - 1],
                send_sem=gsend.at[s, k, 0], recv_sem=grecv.at[s, k, 0],
                device_id=dev(rk), device_id_type=MESH).start()

    def wait_all(s, k, phase):
        buf = rb[s * len(pieces) + k]
        pltpu.make_async_copy(buf, buf, gsend.at[s, k, phase]).wait()
        pltpu.make_async_copy(buf, buf, grecv.at[s, k, phase]).wait()

    def reduce_finish(s, k):
        g, stride = stages[s]
        n = pieces[k] // g
        wait_all(s, k, 0)
        me = (rank // stride) % g
        mine = pl.ds(pl.multiple_of(offs[k] + me * n, 8), n)
        total = gl[s][mine, :]
        for o in range(g - 1):
            total = total + rb[s * len(pieces) + k][o]
        gl[s + 1][mine, :] = total
        for o in range(1, g):
            _, rk = peer(s, o)
            pltpu.make_async_remote_copy(
                src_ref=gl[s + 1].at[mine], dst_ref=gl[s + 1].at[mine],
                send_sem=gsend.at[s, k, 1], recv_sem=grecv.at[s, k, 1],
                device_id=dev(rk), device_id_type=MESH).start()

    wait(ex[0])
    stencil(0, first)
    start(ex[1])

    def gram0(i, acc):
        a = two_rows(f0, i, 1)
        return acc + dot3(a, a, NT)

    gl[0][0:pairs, :] = lax.fori_loop(0, rows // 2, gram0, jnp.zeros((pairs, pairs), F32))
    reduce_start(0, 0)
    wait(ex[1])
    stencil(1, second)
    start(ex[2])

    def gram1(i, acc):
        a, b = two_rows(f0, i, 1), two_rows(f1, i, 1)
        both = tuple(jnp.concatenate([p, q], 0) for p, q in zip(a, b))
        return acc + dot3(both, b, NT)

    reduce_finish(0, 0)
    gl[0][pairs:3 * pairs, :] = lax.fori_loop(0, rows // 2, gram1, jnp.zeros((2 * pairs, pairs), F32))
    reduce_start(0, 1)
    wait(ex[2])
    stencil(2, third)

    def gram2(i, acc):
        return acc + dot3(two_rows(f1, i, 1), two_rows(w2_ref, i, 0), NT)

    gl[0][3 * pairs:, :] = lax.fori_loop(0, rows // 2, gram2, jnp.zeros((pairs, pairs), F32))
    reduce_start(0, 2)
    reduce_finish(0, 1)
    reduce_finish(0, 2)
    for k in range(3):
        wait_all(0, k, 1)
    for s in range(1, nst):
        for k in range(3):
            reduce_start(s, k)
        for k in range(3):
            reduce_finish(s, k)
        for k in range(3):
            wait_all(s, k, 1)
    gram_ref[...] = gl[nst][...]


def mm(a, b):
    return lax.dot_general(a, b, NN, precision=lax.Precision.HIGHEST, preferred_element_type=F32)


def eliminate(systems):
    n = systems[0][0].shape[0]
    state = [list(s) for s in systems]
    lane = lax.broadcasted_iota(jnp.int32, (n, n), 1)
    row = lax.broadcasted_iota(jnp.int32, (n, n), 0)
    sub = lax.broadcasted_iota(jnp.int32, (BLOCK, n), 0)
    for k in range(n // BLOCK):
        lo, hi = k * BLOCK, (k + 1) * BLOCK
        inside = (row >= lo) & (row < hi)
        lhs_mask = (lane >= lo) & (lane < hi) & jnp.logical_not(inside)
        panels = []
        for mats in state:
            pan = [m[lo:hi, :] for m in mats]
            panels.append(([jnp.broadcast_to(pan[0][:, lo + j:lo + j + 1], (BLOCK, n)) for j in range(BLOCK)], pan))
        for i in range(BLOCK):
            for cs, pan in panels:
                f = cs[i]
                rinv = 1.0 / f[i:i + 1, :]

                def step(t):
                    top = t[i:i + 1, :] * rinv
                    return jnp.where(sub == i, top, t - f * top)

                for j in range(i + 1, BLOCK):
                    cs[j] = step(cs[j])
                for q in range(len(pan)):
                    pan[q] = step(pan[q])
        for mats, (_, pan) in zip(state, panels):
            lhs = jnp.where(lhs_mask, mats[0], 0.0)
            for q in range(len(mats)):
                parts = []
                if lo:
                    parts.append(jnp.zeros((lo, n), F32))
                parts.append(pan[q])
                if hi < n:
                    parts.append(jnp.zeros((n - hi, n), F32))
                full = jnp.concatenate(parts, 0)
                mats[q] = jnp.where(inside, full, mats[q] - mm(lhs, full))
    return [s[1:] for s in state]


def finish_kernel(gram_ref, r0_ref, w1_ref, w2_ref, x_ref, out_x, out_r, ch, cl):
    rows, n, cols = r0_ref.shape

    def sym(m):
        return 0.5 * (m + m.T)

    g = sym(gram_ref[0:n, :])
    e = sym(gram_ref[n:2 * n, :])
    f = sym(gram_ref[2 * n:3 * n, :])
    h = sym(gram_ref[3 * n:, :])
    eye = (lax.broadcasted_iota(jnp.int32, (n, n), 0) == lax.broadcasted_iota(jnp.int32, (n, n), 1)).astype(F32)
    (a, ap), (ginv,) = eliminate([(LEAK * g + e, g, e), (g, eye)])
    rr = sym(mm(a.T, mm(f, a) - mm(e, ap)))
    p = ap + mm(ginv, rr)
    curv = sym(mm(a.T, mm(LEAK * f + h, a) - mm(LEAK * e + f, p)))
    ((al,),) = eliminate([(curv, rr)])
    q = mm(a, al)
    pq = mm(p, al)
    zero = jnp.zeros((n, n), F32)
    top = jnp.concatenate([(a + pq).T, -q.T, zero], 1)
    bottom = jnp.concatenate([(ap - LEAK * pq).T, (LEAK * q - a - pq).T, q.T], 1)
    hi, lo = split(jnp.concatenate([top, bottom], 0))
    ch[...] = hi
    cl[...] = lo

    def body(i, carry):
        fh, fl = split(jnp.concatenate(
            [jnp.concatenate([ref[2 * i], ref[2 * i + 1]], 1) for ref in (r0_ref, w1_ref, w2_ref)], 0))
        out = dot3((ch[...], cl[...]), (fh, fl), NN)
        for d in range(2):
            at = pl.ds(2 * i + d, n, stride=rows)
            out_x[at, :] = x_ref[at, :] + out[:n, d * cols:(d + 1) * cols]
            out_r[at, :] = out[n:, d * cols:(d + 1) * cols]
        return carry

    lax.fori_loop(0, rows // 2, body, 0)


def per_device(sizes, land_cover, prune_mask, class_resistance, source_cells, ground_cells, warm_start):
    rows, cols = land_cover.shape
    pairs = warm_start.shape[0]
    pieces = (pairs, 2 * pairs, pairs)
    count = sizes[0] * sizes[1] * sizes[2]
    stages = stages_of(count)
    nst = max(1, len(stages))
    x2d = warm_start.reshape(pairs * rows, cols)
    field = jax.ShapeDtypeStruct((rows, pairs, cols), F32)
    vm = pl.BlockSpec(memory_space=pltpu.VMEM)
    sums = [pltpu.VMEM((4 * pairs, pairs), F32) for _ in range(nst + 1)]
    slots = [pltpu.VMEM((g - 1, n // g, pairs), F32) for g, _ in stages for n in pieces]
    r0, w1, w2, gram = pl.pallas_call(
        functools.partial(krylov_kernel, sizes, pieces),
        out_shape=(field, field, field, jax.ShapeDtypeStruct((4 * pairs, pairs), F32)),
        in_specs=[vm, vm, pl.BlockSpec(memory_space=pltpu.SMEM), vm, vm, vm],
        out_specs=(vm, vm, vm, vm),
        scratch_shapes=[
            pltpu.VMEM((rows + 2, pairs, cols), F32),
            pltpu.VMEM((rows + 2, pairs, cols), F32),
            pltpu.VMEM((rows + 2, pairs, cols), F32),
            pltpu.VMEM((3, pairs, cols), F32),
            pltpu.VMEM((3, pairs, cols), F32),
            pltpu.VMEM((3, pairs, cols), F32),
            pltpu.VMEM((8, cols), F32),
            pltpu.VMEM((8, cols), F32),
            pltpu.VMEM((8, cols), F32),
            pltpu.VMEM((2, rows, cols), F32),
            pltpu.VMEM((2, rows, cols), F32),
            pltpu.VMEM((2, rows, cols), F32),
            pltpu.VMEM((4, rows, cols), F32),
            pltpu.VMEM((2, pairs, cols), F32),
            pltpu.SemaphoreType.DMA((3, 4)),
            pltpu.SemaphoreType.DMA((3, 4)),
            pltpu.SemaphoreType.DMA((4,)),
            pltpu.SemaphoreType.DMA((4,)),
            pltpu.SemaphoreType.DMA((nst, 3, 2)),
            pltpu.SemaphoreType.DMA((nst, 3, 2)),
            *sums, *slots,
        ],
        compiler_params=pltpu.CompilerParams(
            collective_id=0, has_side_effects=True, vmem_limit_bytes=40 * 2**20),
        name="krylov",
    )(land_cover, prune_mask, class_resistance, source_cells.reshape(1, pairs), ground_cells.reshape(1, pairs), x2d)
    flat = jax.ShapeDtypeStruct((pairs * rows, cols), F32)
    pot, resid = pl.pallas_call(
        finish_kernel,
        out_shape=(flat, flat),
        in_specs=[vm] * 5,
        out_specs=(vm, vm),
        scratch_shapes=[pltpu.VMEM((2 * pairs, 3 * pairs), jnp.bfloat16)] * 2,
        compiler_params=pltpu.CompilerParams(vmem_limit_bytes=40 * 2**20),
        name="finish",
    )(gram, r0, w1, w2, x2d)
    return pot.reshape(warm_start.shape), resid.reshape(warm_start.shape)


def solution(mesh):
    in_specs = (
        P(("groups", "wide"), ("narrow", "inner")),
        P(None, ("groups", "wide"), ("narrow", "inner")),
        P(),
        P("groups"),
        P("groups"),
        P(None, ("groups", "wide"), ("narrow", "inner")),
    )
    out_specs = (
        P(None, ("groups", "wide"), ("narrow", "inner")),
        P(None, ("groups", "wide"), ("narrow", "inner")),
    )
    sizes = tuple(mesh.shape[a] for a in ("wide", "narrow", "inner"))
    return jax.shard_map(
        functools.partial(per_device, sizes), mesh=mesh, in_specs=in_specs, out_specs=out_specs, check_vma=False
    )
```

time: 450 us -> 65.1 us (0.14); the launches traced: 442 us -> 64.8 us
  waiting for transfers between devices: 259 us -> 0 us
  other arithmetic: 74.6 us -> 0 us
  Pallas kernels: 0 us -> 59.3 us
  starting transfers between devices: 46.2 us -> 0 us
  matrix products: 33.8 us -> 0 us
  between operations: 14.7 us -> 0.66 us
  local copies, waits for them, and re-layouts: 13.2 us -> 4.81 us
    psum x3 -> x0, waiting for transfers between devices: 253 us -> none  [the longest x2 166 us: per_device(): lax.psum(gram(residual, residual), ('wide', 'narrow', 'inner'))]
    another operation x15 -> x0, other arithmetic: 68.5 us -> none  [the longest x9 37.2 us: spd_solve(): factor = jnp.linalg.cholesky(matrix)]
    pallas_call x0 -> x2, Pallas kernels: none -> 59.3 us  [the longest x1 42.9 us: per_device(): pl.pallas_call(functools.partial(krylov_kernel, sizes, pieces), out_shape...]
    ppermute x16 -> x0, starting transfers between devices: 45.8 us -> none  [the longest x6 29 us: with_halo(): lax.ppermute(lax.slice_in_dim(block, block.shape[dim] - width, None, axis...]
    dot_general x9 -> x0, matrix products: 31.4 us -> none  [the longest x4 16.4 us: gram(): jnp.dot(left.reshape(count, -1), right.reshape(count, -1).T, precision=la...]
    ppermute x16 -> x0, waiting for transfers between devices: 5.9 us -> none  [the longest x6 4.56 us: with_halo(): lax.ppermute(lax.slice_in_dim(block, block.shape[dim] - width, None, axis...]
  transfers between devices with their start and end apart: 19 -> 0, of which waited for: 10 -> 0; matrix products, arithmetic and copies ran while one was open for 4% -> 0% of each run, Pallas kernels for 0% -> 0%
where the time goes in v1:
time: 65.1 us; the launch traced here: 64.8 us
  Pallas kernels  59.3 us (91%)
  local copies, waits for them, and re-layouts  4.81 us (7%)
  between operations  0.66 us (1%)
    pallas_call x1, Pallas kernels, per_device(): pl.pallas_call(functools.partial(krylov_kernel, sizes, pieces), out_shape...  42.9 us
    pallas_call x1, Pallas kernels, per_device(): pl.pallas_call(finish_kernel, out_shape=(flat, flat), in_specs=[vm] * 5,...  16.5 us
    unnamed x14, local copies, waits for them, and re-layouts  4.81 us

profile of v1, /device:TPU:0, one launch (start us, length us, event | category | flops | bytes accessed | tf_op | source)
XLA Modules:
  0.0 64.8 jit_solution(1098162362060896993)
XLA Ops:
  0.6 0.0 copy-start
  0.6 1.4 %copy-done = f32[128,24,128]{2,1,0:T(8,128)S(1)} copy-done((f32[128,24,128]{2,1,0:T(8,128)S(1)}, f32[128,24,128]{2,1,0:T(8,128)}, u32[]{:S(2)}) %copy-start) | copy-done | bytes 1572888
  2.0 0.0 copy-start.2
  2.0 0.7 %copy-done.2 = s32[2,24,128]{2,1,0:T(8,128)S(1)} copy-done((s32[2,24,128]{2,1,0:T(8,128)S(1)}, s32[2,24,128]{2,1,0:T(8,128)}, u32[]{:S(2)}) %copy-start.2) | copy-done | bytes 24600
  2.8 0.0 copy-start.3
  2.8 0.7 %copy-done.3 = s32[24,128]{1,0:T(8,128)S(1)} copy-done((s32[24,128]{1,0:T(8,128)S(1)}, s32[24,128]{1,0:T(8,128)}, u32[]{:S(2)}) %copy-start.3) | copy-done | bytes 12312
  3.5 0.0 copy-start.4
  3.5 0.7 %copy-done.4 = f32[16]{0:T(128)S(1)} copy-done((f32[16]{0:T(128)S(1)}, f32[16]{0:T(128)}, u32[]{:S(2)}) %copy-start.4) | copy-done | bytes 88
  4.1 0.0 copy-start.5
  4.1 0.7 %copy-done.5 = s32[128]{0:T(128)S(1)} copy-done((s32[128]{0:T(128)S(1)}, s32[128]{0:T(128)}, u32[]{:S(2)}) %copy-start.5) | copy-done | bytes 536
  4.8 0.0 copy-start.6
  4.8 0.7 %copy-done.6 = s32[128]{0:T(128)S(1)} copy-done((s32[128]{0:T(128)S(1)}, s32[128]{0:T(128)}, u32[]{:S(2)}) %copy-start.6) | copy-done | bytes 536
  5.5 0.0 copy-start.1
  5.5 42.9 %krylov.1 = (f32[24,128,128]{2,1,0:T(8,128)S(1)}, f32[24,128,128]{2,1,0:T(8,128)S(1)}, f32[24,128,128]{2,1,0:T(8,128)S(1)}, f32[512,128]{1,0:T(8,128)S(1)}) custom-call(s32[24,128]{1,0:T(8,128)S(1)} %copy-done.3, s32[2,24,128]{2,1,0:T(8,128)S(1)} %copy-done.2, f32[16]{0:T(128)S(1)} %copy-done.4, s32[1,128]{1,0:T(1,128)S(1)} %bitcast.7, ...), custom_call_target="tpu_custom_call" | custom-call | tf_op jit(solution)/shard_map/krylov/pallas_call | solution.py:409
  48.3 0.0 copy-done.1
  48.3 16.5 %finish.1 = (f32[3072,128]{1,0:T(8,128)}, f32[3072,128]{1,0:T(8,128)}) custom-call(f32[512,128]{1,0:T(8,128)S(1)} %get-tuple-element.8.gram_ref, f32[24,128,128]{2,1,0:T(8,128)S(1)} %get-tuple-element.9.r0_ref, f32[24,128,128]{2,1,0:T(8,128)S(1)} %get-tuple-element.10.w1_ref, f32[24,128,128]{2,1,0:T(8,128)S(1)} %get-tuple-element.11.w2_ref, ...), custom_call_target="tpu_custom_call" | custom-call | tf_op jit(solution)/shard_map/finish/pallas_call | solution.py:442
Async XLA Ops:
  0.6 1.4 %copy-start = (f32[128,24,128]{2,1,0:T(8,128)S(1)}, f32[128,24,128]{2,1,0:T(8,128)}, u32[]{:S(2)}) copy-start(f32[128,24,128]{2,1,0:T(8,128)} %param.11) | copy-start | bytes 4718596
  2.0 0.7 %copy-start.2 = (s32[2,24,128]{2,1,0:T(8,128)S(1)}, s32[2,24,128]{2,1,0:T(8,128)}, u32[]{:S(2)}) copy-start(s32[2,24,128]{2,1,0:T(8,128)} %prune_ref.1) | copy-start | bytes 73732
  2.8 0.7 %copy-start.3 = (s32[24,128]{1,0:T(8,128)S(1)}, s32[24,128]{1,0:T(8,128)}, u32[]{:S(2)}) copy-start(s32[24,128]{1,0:T(8,128)} %cover_ref.1) | copy-start | bytes 36868
  3.5 0.7 %copy-start.4 = (f32[16]{0:T(128)S(1)}, f32[16]{0:T(128)}, u32[]{:S(2)}) copy-start(f32[16]{0:T(128)} %table_ref.1) | copy-start | bytes 196
  4.1 0.7 %copy-start.5 = (s32[128]{0:T(128)S(1)}, s32[128]{0:T(128)}, u32[]{:S(2)}) copy-start(s32[128]{0:T(128)} %param.9) | copy-start | bytes 1540
  4.8 0.7 %copy-start.6 = (s32[128]{0:T(128)S(1)}, s32[128]{0:T(128)}, u32[]{:S(2)}) copy-start(s32[128]{0:T(128)} %param.10) | copy-start | bytes 1540
  5.5 42.9 %copy-start.1 = (f32[128,24,128]{2,1,0:T(8,128)S(1)}, f32[128,24,128]{2,1,0:T(8,128)}, u32[]{:S(2)}) copy-start(f32[128,24,128]{2,1,0:T(8,128)} %param.11) | copy-start | bytes 4718596

commit v2 on v1

--- a/solution.py
+++ b/solution.py
@@ -11,6 +11,7 @@
 F32 = jnp.float32
 GROUP = 16
 BLOCK = 16
+STEP = 4
 NT = (((1,), (1,)), ((), ()))
 NN = (((1,), (0,)), ((), ()))
 
@@ -37,9 +38,9 @@
     return out
 
 
-def krylov_kernel(sizes, pieces, cover_ref, prune_ref, table_ref, src_ref, gnd_ref, x_ref,
-                  r0_ref, w1_ref, w2_ref, gram_ref,
-                  fx, f0, f1, packs, lefts, rights, edge, edge_up, edge_down, side, side_left, side_right,
+def krylov_kernel(sizes, pieces, cover_hbm, prune_hbm, table_hbm, src_hbm, gnd_hbm, x_hbm,
+                  vh, vl, gram_ref,
+                  cover_ref, prune_ref, table_ref, src_ref, gnd_ref, x_ref, insem, fx, f0, f1, packs, lefts, rights, edge, edge_up, edge_down, side, side_left, side_right,
                   cond, sg, hsend, hrecv, isend, irecv, gsend, grecv, *bufs):
     wide_n, narrow_n, inner_n = sizes
     pairs = fx.shape[1]
@@ -63,6 +64,11 @@
         other = (digit + o) % g
         return other, rank + (other - digit) * stride
 
+    loads = [pltpu.make_async_copy(a, b, insem.at[i]) for i, (a, b) in enumerate((
+        (x_hbm, x_ref), (cover_hbm, cover_ref), (prune_hbm, prune_ref), (table_hbm, table_ref),
+        (src_hbm, src_ref), (gnd_hbm, gnd_ref)))]
+    for cp in loads:
+        cp.start()
     barrier = pltpu.get_barrier_semaphore()
     expect = 0
     for s, (g, _) in enumerate(stages):
@@ -82,6 +88,8 @@
     half = pairs // 2
     lane_h = lax.broadcasted_iota(jnp.int32, (half, cols), 1)
 
+    for cp in loads[1:4]:
+        cp.wait()
     cover = cover_ref[...]
     res = jnp.zeros((rows, cols), F32)
     for k in range(table_ref.shape[0]):
@@ -108,15 +116,20 @@
             ref[...] = jnp.ones(ref.shape, F32)
 
     packs[0] = zero_row
-
-    def load_row(r, carry):
-        v = x_ref[pl.ds(r, pairs, stride=rows), :]
-        fx[r + 1] = v
-        rolled = pltpu.roll(v, 2 * r, 1)
-        packs[0] = jnp.where((lane == 2 * r) | (lane == (2 * r + cols - 1) % cols), rolled, packs[0])
+    loads[0].wait()
+
+    def load_rows(i, carry):
+        pack = packs[0]
+        for d in range(STEP):
+            r = i * STEP + d
+            v = x_ref[pl.ds(r, pairs, stride=rows), :]
+            fx[r + 1] = v
+            rolled = pltpu.roll(v, 2 * r, 1)
+            pack = jnp.where((lane == 2 * r) | (lane == (2 * r + cols - 1) % cols), rolled, pack)
+        packs[0] = pack
         return carry
 
-    lax.fori_loop(0, rows, load_row, 0)
+    lax.fori_loop(0, rows // STEP, load_rows, 0)
     pl.semaphore_wait(barrier, expect + near)
 
     def halo(e):
@@ -158,6 +171,8 @@
     ex = [copies(halo(e), hsend.at[e], hrecv.at[e]) for e in range(3)]
     start(ex[0])
 
+    for cp in loads[4:]:
+        cp.wait()
     src_t = jnp.broadcast_to(src_ref[...].astype(F32), (cols, pairs)).T
     gnd_t = jnp.broadcast_to(gnd_ref[...].astype(F32), (cols, pairs)).T
     sg[0] = src_t
@@ -188,23 +203,34 @@
         if e < 2:
             packs[e + 1] = zero_row
 
-        def body(r, carry):
-            cr, cl, cd, cu = (cond[k, pl.ds(r, 1), :] for k in range(4))
+        def body(i, carry):
             for h in range(2):
                 hs = pl.ds(h * half, half)
-                v = field[r + 1, hs, :]
-                edges = pltpu.roll(lefts[e, hs, :], (2 * cols - 2 * r - 1) % cols, 1)
-                xr = jnp.where(lane_h == cols - 1, edges, pltpu.roll(v, cols - 1, 1))
-                xl = jnp.where(lane_h == 0, edges, pltpu.roll(v, 1, 1))
-                lap = cr * (v - xr) + cl * (v - xl) + cd * (v - field[r + 2, hs, :]) + cu * (v - field[r, hs, :])
-                out = finish(r, hs, v, lap)
+                halos = lefts[e, hs, :]
+                pack = packs[e + 1, hs, :] if e < 2 else None
+                for d in range(STEP):
+                    r = i * STEP + d
+                    cr, cl, cd, cu = (cond[k, pl.ds(r, 1), :] for k in range(4))
+                    v = field[r + 1, hs, :]
+                    edges = pltpu.roll(halos, (2 * cols - 2 * r - 1) % cols, 1)
+                    xr = jnp.where(lane_h == cols - 1, edges, pltpu.roll(v, cols - 1, 1))
+                    xl = jnp.where(lane_h == 0, edges, pltpu.roll(v, 1, 1))
+                    lap = cr * (v - xr) + cl * (v - xl) + cd * (v - field[r + 2, hs, :]) + cu * (v - field[r, hs, :])
+                    out = finish(r, hs, v, lap)
+                    if e < 2:
+                        (f0, f1)[e][r + 1, hs, :] = out
+                        rolled = pltpu.roll(out, 2 * r, 1)
+                        pack = jnp.where(
+                            (lane_h == 2 * r) | (lane_h == (2 * r + cols - 1) % cols), rolled, pack)
+                    at = (pl.ds(e * pairs + h * half, half), pl.ds(pl.multiple_of(r * cols, cols), cols))
+                    hi, lo = split(out)
+                    vh[at] = hi
+                    vl[at] = lo
                 if e < 2:
-                    rolled = pltpu.roll(out, 2 * r, 1)
-                    packs[e + 1, hs, :] = jnp.where(
-                        (lane_h == 2 * r) | (lane_h == (2 * r + cols - 1) % cols), rolled, packs[e + 1, hs, :])
+                    packs[e + 1, hs, :] = pack
             return carry
 
-        lax.fori_loop(0, rows, body, 0)
+        lax.fori_loop(0, rows // STEP, body, 0)
 
     total_cols = cols * cells_n
     col_f = (lax.broadcasted_iota(jnp.int32, (1, cols), 1) + c * cols)
@@ -213,21 +239,13 @@
         flat = (col_f + (w * rows + r) * total_cols).astype(F32)
         cur = (sg[0, hs, :] == flat).astype(F32) - (sg[1, hs, :] == flat).astype(F32)
         out = cur - (LEAK * v + lap)
-        f0[r + 1, hs, :] = out
-        r0_ref[r, hs, :] = out
         return out
 
     def second(r, hs, v, lap):
-        f1[r + 1, hs, :] = lap
-        w1_ref[r, hs, :] = lap
         return lap
 
-    def third(r, hs, v, lap):
-        w2_ref[r, hs, :] = lap
-        return lap
-
-    def two_rows(ref, i, off):
-        return split(jnp.concatenate([ref[2 * i + off], ref[2 * i + 1 + off]], 1))
+    def part(lo, hi):
+        return vh[lo * pairs:hi * pairs, :], vl[lo * pairs:hi * pairs, :]
 
     nst = len(stages)
     gl = bufs[:nst + 1]
@@ -271,31 +289,19 @@
     stencil(0, first)
     start(ex[1])
 
-    def gram0(i, acc):
-        a = two_rows(f0, i, 1)
-        return acc + dot3(a, a, NT)
-
-    gl[0][0:pairs, :] = lax.fori_loop(0, rows // 2, gram0, jnp.zeros((pairs, pairs), F32))
+    gl[0][0:pairs, :] = dot3(part(0, 1), part(0, 1), NT)
     reduce_start(0, 0)
     wait(ex[1])
     stencil(1, second)
     start(ex[2])
 
-    def gram1(i, acc):
-        a, b = two_rows(f0, i, 1), two_rows(f1, i, 1)
-        both = tuple(jnp.concatenate([p, q], 0) for p, q in zip(a, b))
-        return acc + dot3(both, b, NT)
-
     reduce_finish(0, 0)
-    gl[0][pairs:3 * pairs, :] = lax.fori_loop(0, rows // 2, gram1, jnp.zeros((2 * pairs, pairs), F32))
+    gl[0][pairs:3 * pairs, :] = dot3(part(0, 2), part(1, 2), NT)
     reduce_start(0, 1)
     wait(ex[2])
-    stencil(2, third)
-
-    def gram2(i, acc):
-        return acc + dot3(two_rows(f1, i, 1), two_rows(w2_ref, i, 0), NT)
-
-    gl[0][3 * pairs:, :] = lax.fori_loop(0, rows // 2, gram2, jnp.zeros((pairs, pairs), F32))
+    stencil(2, second)
+
+    gl[0][3 * pairs:, :] = dot3(part(1, 2), part(2, 3), NT)
     reduce_start(0, 2)
     reduce_finish(0, 1)
     reduce_finish(0, 2)
@@ -356,8 +362,11 @@
     return [s[1:] for s in state]
 
 
-def finish_kernel(gram_ref, r0_ref, w1_ref, w2_ref, x_ref, out_x, out_r, ch, cl):
-    rows, n, cols = r0_ref.shape
+def finish_kernel(gram_ref, vh, vl, x_hbm, out_x, out_r, x_ref, bx, br, ch, cl, insem, outsem):
+    groups, n, tile, cols = bx.shape
+    rows = groups * tile
+    load = pltpu.make_async_copy(x_hbm, x_ref, insem)
+    load.start()
 
     def sym(m):
         return 0.5 * (m + m.T)
@@ -381,17 +390,24 @@
     ch[...] = hi
     cl[...] = lo
 
-    def body(i, carry):
-        fh, fl = split(jnp.concatenate(
-            [jnp.concatenate([ref[2 * i], ref[2 * i + 1]], 1) for ref in (r0_ref, w1_ref, w2_ref)], 0))
-        out = dot3((ch[...], cl[...]), (fh, fl), NN)
-        for d in range(2):
-            at = pl.ds(2 * i + d, n, stride=rows)
-            out_x[at, :] = x_ref[at, :] + out[:n, d * cols:(d + 1) * cols]
-            out_r[at, :] = out[n:, d * cols:(d + 1) * cols]
-        return carry
-
-    lax.fori_loop(0, rows // 2, body, 0)
+    load.wait()
+    stores = []
+    for g in range(groups):
+        for i in range(tile // 2):
+            at = pl.ds((g * tile + 2 * i) * cols, 2 * cols)
+            out = dot3((ch[...], cl[...]), (vh[:, at], vl[:, at]), NN)
+            for d in range(2):
+                r = 2 * i + d
+                here = pl.ds(r, n, stride=tile)
+                bx.at[g].reshape(n * tile, cols)[here, :] = (
+                    x_ref[pl.ds(g * tile + r, n, stride=rows), :] + out[:n, d * cols:(d + 1) * cols])
+                br.at[g].reshape(n * tile, cols)[here, :] = out[n:, d * cols:(d + 1) * cols]
+        for j, (buf, dst) in enumerate(((bx, out_x), (br, out_r))):
+            cp = pltpu.make_async_copy(buf.at[g], dst.at[:, pl.ds(g * tile, tile), :], outsem.at[j, g])
+            cp.start()
+            stores.append(cp)
+    for cp in stores:
+        cp.wait()
 
 
 def per_device(sizes, land_cover, prune_mask, class_resistance, source_cells, ground_cells, warm_start):
@@ -402,16 +418,24 @@
     stages = stages_of(count)
     nst = max(1, len(stages))
     x2d = warm_start.reshape(pairs * rows, cols)
-    field = jax.ShapeDtypeStruct((rows, pairs, cols), F32)
+    basis = jax.ShapeDtypeStruct((3 * pairs, rows * cols), jnp.bfloat16)
+    hbm = pl.BlockSpec(memory_space=pltpu.HBM)
     vm = pl.BlockSpec(memory_space=pltpu.VMEM)
     sums = [pltpu.VMEM((4 * pairs, pairs), F32) for _ in range(nst + 1)]
     slots = [pltpu.VMEM((g - 1, n // g, pairs), F32) for g, _ in stages for n in pieces]
-    r0, w1, w2, gram = pl.pallas_call(
+    vh, vl, gram = pl.pallas_call(
         functools.partial(krylov_kernel, sizes, pieces),
-        out_shape=(field, field, field, jax.ShapeDtypeStruct((4 * pairs, pairs), F32)),
-        in_specs=[vm, vm, pl.BlockSpec(memory_space=pltpu.SMEM), vm, vm, vm],
-        out_specs=(vm, vm, vm, vm),
+        out_shape=(basis, basis, jax.ShapeDtypeStruct((4 * pairs, pairs), F32)),
+        in_specs=[hbm] * 6,
+        out_specs=(vm, vm, vm),
         scratch_shapes=[
+            pltpu.VMEM((rows, cols), jnp.int32),
+            pltpu.VMEM((2, rows, cols), jnp.int32),
+            pltpu.SMEM(class_resistance.shape, F32),
+            pltpu.VMEM((1, pairs), jnp.int32),
+            pltpu.VMEM((1, pairs), jnp.int32),
+            pltpu.VMEM((pairs * rows, cols), F32),
+            pltpu.SemaphoreType.DMA((6,)),
             pltpu.VMEM((rows + 2, pairs, cols), F32),
             pltpu.VMEM((rows + 2, pairs, cols), F32),
             pltpu.VMEM((rows + 2, pairs, cols), F32),
@@ -438,17 +462,25 @@
             collective_id=0, has_side_effects=True, vmem_limit_bytes=40 * 2**20),
         name="krylov",
     )(land_cover, prune_mask, class_resistance, source_cells.reshape(1, pairs), ground_cells.reshape(1, pairs), x2d)
-    flat = jax.ShapeDtypeStruct((pairs * rows, cols), F32)
-    pot, resid = pl.pallas_call(
+    full = jax.ShapeDtypeStruct(warm_start.shape, F32)
+    tile = 8
+    return pl.pallas_call(
         finish_kernel,
-        out_shape=(flat, flat),
-        in_specs=[vm] * 5,
-        out_specs=(vm, vm),
-        scratch_shapes=[pltpu.VMEM((2 * pairs, 3 * pairs), jnp.bfloat16)] * 2,
+        out_shape=(full, full),
+        in_specs=[vm, vm, vm, hbm],
+        out_specs=(hbm, hbm),
+        scratch_shapes=[
+            pltpu.VMEM((pairs * rows, cols), F32),
+            pltpu.VMEM((rows // tile, pairs, tile, cols), F32),
+            pltpu.VMEM((rows // tile, pairs, tile, cols), F32),
+            pltpu.VMEM((2 * pairs, 3 * pairs), jnp.bfloat16),
+            pltpu.VMEM((2 * pairs, 3 * pairs), jnp.bfloat16),
+            pltpu.SemaphoreType.DMA,
+            pltpu.SemaphoreType.DMA((2, rows // tile)),
+        ],
         compiler_params=pltpu.CompilerParams(vmem_limit_bytes=40 * 2**20),
         name="finish",
-    )(gram, r0, w1, w2, x2d)
-    return pot.reshape(warm_start.shape), resid.reshape(warm_start.shape)
+    )(gram, vh, vl, x2d)
 
 
 def solution(mesh):

time: 65.1 us -> 58.2 us (0.89)
  Pallas kernels: 59.3 us -> 52.3 us
    pallas_call x1, Pallas kernels: 42.9 us -> 37.7 us  [per_device(): pl.pallas_call(functools.partial(krylov_kernel, sizes, pieces), out_shape...]
    pallas_call x1, Pallas kernels: 16.5 us -> 14.5 us  [per_device(): pl.pallas_call(finish_kernel, out_shape=(full, full), in_specs=[vm, vm, v...]
where the time goes in v2:
time: 58.2 us; the launch traced here: 57.9 us
  Pallas kernels  52.3 us (90%)
  local copies, waits for them, and re-layouts  4.81 us (8%)
  between operations  0.82 us (1%)
    pallas_call x1, Pallas kernels, per_device(): pl.pallas_call(functools.partial(krylov_kernel, sizes, pieces), out_shape...  37.7 us
    pallas_call x1, Pallas kernels, per_device(): pl.pallas_call(finish_kernel, out_shape=(full, full), in_specs=[vm, vm, v...  14.5 us
    unnamed x14, local copies, waits for them, and re-layouts  4.81 us

profile of v2, /device:TPU:0, one launch (start us, length us, event | category | flops | bytes accessed | tf_op | source)
XLA Modules:
  0.0 57.9 jit_solution(10895447052523255154)
XLA Ops:
  0.6 0.0 copy-start
  0.6 1.4 %copy-done = f32[128,24,128]{2,1,0:T(8,128)S(1)} copy-done((f32[128,24,128]{2,1,0:T(8,128)S(1)}, f32[128,24,128]{2,1,0:T(8,128)}, u32[]{:S(2)}) %copy-start) | copy-done | bytes 1572888
  2.0 0.0 copy-start.2
  2.0 0.7 %copy-done.2 = s32[2,24,128]{2,1,0:T(8,128)S(1)} copy-done((s32[2,24,128]{2,1,0:T(8,128)S(1)}, s32[2,24,128]{2,1,0:T(8,128)}, u32[]{:S(2)}) %copy-start.2) | copy-done | bytes 24600
  2.8 0.0 copy-start.3
  2.8 0.7 %copy-done.3 = s32[24,128]{1,0:T(8,128)S(1)} copy-done((s32[24,128]{1,0:T(8,128)S(1)}, s32[24,128]{1,0:T(8,128)}, u32[]{:S(2)}) %copy-start.3) | copy-done | bytes 12312
  3.5 0.0 copy-start.4
  3.5 0.7 %copy-done.4 = f32[16]{0:T(128)S(1)} copy-done((f32[16]{0:T(128)S(1)}, f32[16]{0:T(128)}, u32[]{:S(2)}) %copy-start.4) | copy-done | bytes 88
  4.1 0.0 copy-start.5
  4.1 0.7 %copy-done.5 = s32[128]{0:T(128)S(1)} copy-done((s32[128]{0:T(128)S(1)}, s32[128]{0:T(128)}, u32[]{:S(2)}) %copy-start.5) | copy-done | bytes 536
  4.8 0.0 copy-start.6
  4.8 0.7 %copy-done.6 = s32[128]{0:T(128)S(1)} copy-done((s32[128]{0:T(128)S(1)}, s32[128]{0:T(128)}, u32[]{:S(2)}) %copy-start.6) | copy-done | bytes 536
  5.5 0.0 copy-start.1
  5.5 37.7 %krylov.1 = (bf16[384,3072]{1,0:T(8,128)(2,1)S(1)}, bf16[384,3072]{1,0:T(8,128)(2,1)S(1)}, f32[512,128]{1,0:T(8,128)S(1)}) custom-call(s32[24,128]{1,0:T(8,128)S(1)} %copy-done.3, s32[2,24,128]{2,1,0:T(8,128)S(1)} %copy-done.2, f32[16]{0:T(128)S(1)} %copy-done.4, s32[1,128]{1,0:T(1,128)S(1)} %bitcast.5, s32[1,128]{1,0:T(1,128)S(1)} %bitcast.6, ...), custom_call_target="tpu_custom_call" | custom-call | tf_op jit(solution)/shard_map/krylov/pallas_call | solution.py:426
  43.2 0.0 copy-done.1
  43.2 14.5 %finish.1 = (f32[128,24,128]{2,1,0:T(8,128)}, f32[128,24,128]{2,1,0:T(8,128)}) custom-call(f32[512,128]{1,0:T(8,128)S(1)} %get-tuple-element.5.gram_ref, bf16[384,3072]{1,0:T(8,128)(2,1)S(1)} %get-tuple-element.6.vh, bf16[384,3072]{1,0:T(8,128)(2,1)S(1)} %get-tuple-element.7.vl, f32[3072,128]{1,0:T(8,128)S(1)} %bitcast.4), custom_call_target="tpu_custom_call" | custom-call | tf_op jit(solution)/shard_map/finish/pallas_call | solution.py:467
Async XLA Ops:
  0.6 1.4 %copy-start = (f32[128,24,128]{2,1,0:T(8,128)S(1)}, f32[128,24,128]{2,1,0:T(8,128)}, u32[]{:S(2)}) copy-start(f32[128,24,128]{2,1,0:T(8,128)} %param.11) | copy-start | bytes 4718596
  2.0 0.7 %copy-start.2 = (s32[2,24,128]{2,1,0:T(8,128)S(1)}, s32[2,24,128]{2,1,0:T(8,128)}, u32[]{:S(2)}) copy-start(s32[2,24,128]{2,1,0:T(8,128)} %prune_hbm.1) | copy-start | bytes 73732
  2.8 0.7 %copy-start.3 = (s32[24,128]{1,0:T(8,128)S(1)}, s32[24,128]{1,0:T(8,128)}, u32[]{:S(2)}) copy-start(s32[24,128]{1,0:T(8,128)} %cover_hbm.1) | copy-start | bytes 36868
  3.5 0.7 %copy-start.4 = (f32[16]{0:T(128)S(1)}, f32[16]{0:T(128)}, u32[]{:S(2)}) copy-start(f32[16]{0:T(128)} %table_hbm.1) | copy-start | bytes 196
  4.1 0.7 %copy-start.5 = (s32[128]{0:T(128)S(1)}, s32[128]{0:T(128)}, u32[]{:S(2)}) copy-start(s32[128]{0:T(128)} %param.9) | copy-start | bytes 1540
  4.8 0.7 %copy-start.6 = (s32[128]{0:T(128)S(1)}, s32[128]{0:T(128)}, u32[]{:S(2)}) copy-start(s32[128]{0:T(128)} %param.10) | copy-start | bytes 1540
  5.5 37.7 %copy-start.1 = (f32[128,24,128]{2,1,0:T(8,128)S(1)}, f32[128,24,128]{2,1,0:T(8,128)}, u32[]{:S(2)}) copy-start(f32[128,24,128]{2,1,0:T(8,128)} %param.11) | copy-start | bytes 4718596

commit v3 on v2

--- a/solution.py
+++ b/solution.py
@@ -86,7 +86,6 @@
 
     lane = lax.broadcasted_iota(jnp.int32, (pairs, cols), 1)
     half = pairs // 2
-    lane_h = lax.broadcasted_iota(jnp.int32, (half, cols), 1)
 
     for cp in loads[1:4]:
         cp.wait()
@@ -116,6 +115,9 @@
             ref[...] = jnp.ones(ref.shape, F32)
 
     packs[0] = zero_row
+    lane_r = lax.broadcasted_iota(jnp.int32, (rows, cols), 1)
+    row_r = lax.broadcasted_iota(jnp.int32, (rows, cols), 0)
+    cond[5] = ((lane_r == 2 * row_r) | (lane_r == (2 * row_r + cols - 1) % cols)).astype(F32)
     loads[0].wait()
 
     def load_rows(i, carry):
@@ -124,8 +126,7 @@
             r = i * STEP + d
             v = x_ref[pl.ds(r, pairs, stride=rows), :]
             fx[r + 1] = v
-            rolled = pltpu.roll(v, 2 * r, 1)
-            pack = jnp.where((lane == 2 * r) | (lane == (2 * r + cols - 1) % cols), rolled, pack)
+            pack = pack + pltpu.roll(v, 2 * r, 1) * cond[5, pl.ds(r, 1), :]
         packs[0] = pack
         return carry
 
@@ -179,8 +180,6 @@
     sg[1] = gnd_t
 
     wait(info)
-    lane_r = lax.broadcasted_iota(jnp.int32, (rows, cols), 1)
-    row_r = lax.broadcasted_iota(jnp.int32, (rows, cols), 0)
     right_res = jnp.where(lane_r == cols - 1, pltpu.roll(side_right[0], cols - 1, 1), pltpu.roll(res, cols - 1, 1))
     left_res = jnp.where(lane_r == 0, pltpu.roll(side_left[0], 1, 1), pltpu.roll(res, 1, 1))
     left_keep = jnp.where(lane_r == 0, pltpu.roll(side_left[1], 1, 1), pltpu.roll(keep_r, 1, 1))
@@ -191,8 +190,11 @@
     at_left = (lane_r == 0) & jnp.logical_not(has_left)
     at_down = (row_r == rows - 1) & jnp.logical_not(has_down)
     at_up = (row_r == 0) & jnp.logical_not(has_up)
-    cond[0] = jnp.where(at_right, 0.0, keep_r * 2.0 / (res + right_res))
-    cond[1] = jnp.where(at_left, 0.0, left_keep * 2.0 / (res + left_res))
+    to_right = jnp.where(at_right, 0.0, keep_r * 2.0 / (res + right_res))
+    to_left = jnp.where(at_left, 0.0, left_keep * 2.0 / (res + left_res))
+    cond[0] = jnp.where(lane_r == cols - 1, 0.0, to_right)
+    cond[1] = jnp.where(lane_r == 0, 0.0, to_left)
+    cond[4] = jnp.where(lane_r == cols - 1, to_right, jnp.where(lane_r == 0, to_left, 0.0))
     cond[2] = jnp.where(at_down, 0.0, keep_d * 2.0 / (res + down_res))
     cond[3] = jnp.where(at_up, 0.0, up_keep * 2.0 / (res + up_res))
 
@@ -210,18 +212,16 @@
                 pack = packs[e + 1, hs, :] if e < 2 else None
                 for d in range(STEP):
                     r = i * STEP + d
-                    cr, cl, cd, cu = (cond[k, pl.ds(r, 1), :] for k in range(4))
+                    cr, cl, cd, cu, ce, pm = (cond[k, pl.ds(r, 1), :] for k in range(6))
                     v = field[r + 1, hs, :]
                     edges = pltpu.roll(halos, (2 * cols - 2 * r - 1) % cols, 1)
-                    xr = jnp.where(lane_h == cols - 1, edges, pltpu.roll(v, cols - 1, 1))
-                    xl = jnp.where(lane_h == 0, edges, pltpu.roll(v, 1, 1))
-                    lap = cr * (v - xr) + cl * (v - xl) + cd * (v - field[r + 2, hs, :]) + cu * (v - field[r, hs, :])
+                    xr = pltpu.roll(v, cols - 1, 1)
+                    xl = pltpu.roll(v, 1, 1)
+                    lap = cr * (v - xr) + cl * (v - xl) + ce * (v - edges) + cd * (v - field[r + 2, hs, :]) + cu * (v - field[r, hs, :])
                     out = finish(r, hs, v, lap)
                     if e < 2:
                         (f0, f1)[e][r + 1, hs, :] = out
-                        rolled = pltpu.roll(out, 2 * r, 1)
-                        pack = jnp.where(
-                            (lane_h == 2 * r) | (lane_h == (2 * r + cols - 1) % cols), rolled, pack)
+                        pack = pack + pltpu.roll(out, 2 * r, 1) * pm
                     at = (pl.ds(e * pairs + h * half, half), pl.ds(pl.multiple_of(r * cols, cols), cols))
                     hi, lo = split(out)
                     vh[at] = hi
@@ -301,9 +301,9 @@
     wait(ex[2])
     stencil(2, second)
 
+    reduce_finish(0, 1)
     gl[0][3 * pairs:, :] = dot3(part(1, 2), part(2, 3), NT)
     reduce_start(0, 2)
-    reduce_finish(0, 1)
     reduce_finish(0, 2)
     for k in range(3):
         wait_all(0, k, 1)
@@ -321,18 +321,35 @@
     return lax.dot_general(a, b, NN, precision=lax.Precision.HIGHEST, preferred_element_type=F32)
 
 
+def split3(x):
+    h1 = x.astype(jnp.bfloat16)
+    rest = x - h1.astype(F32)
+    h2 = rest.astype(jnp.bfloat16)
+    return h1, h2, (rest - h2.astype(F32)).astype(jnp.bfloat16)
+
+
 def eliminate(systems):
     n = systems[0][0].shape[0]
     state = [list(s) for s in systems]
     lane = lax.broadcasted_iota(jnp.int32, (n, n), 1)
     row = lax.broadcasted_iota(jnp.int32, (n, n), 0)
     sub = lax.broadcasted_iota(jnp.int32, (BLOCK, n), 0)
+    slot = lane // BLOCK
+    second, third = (slot == 2) | (slot == 5), slot == 4
+    assert n == 8 * BLOCK
     for k in range(n // BLOCK):
         lo, hi = k * BLOCK, (k + 1) * BLOCK
         inside = (row >= lo) & (row < hi)
         lhs_mask = (lane >= lo) & (lane < hi) & jnp.logical_not(inside)
-        panels = []
+        panels, lefts = [], []
         for mats in state:
+            t = jnp.where(lhs_mask, mats[0], 0.0)
+            for shift in (BLOCK, 2 * BLOCK, 4 * BLOCK):
+                t = t + pltpu.roll(t, shift, 1)
+            h1 = t.astype(jnp.bfloat16).astype(F32)
+            h2 = (t - h1).astype(jnp.bfloat16).astype(F32)
+            h3 = t - h1 - h2
+            lefts.append(jnp.where(third, h3, jnp.where(second, h2, h1)).astype(jnp.bfloat16))
             pan = [m[lo:hi, :] for m in mats]
             panels.append(([jnp.broadcast_to(pan[0][:, lo + j:lo + j + 1], (BLOCK, n)) for j in range(BLOCK)], pan))
         for i in range(BLOCK):
@@ -348,17 +365,18 @@
                     cs[j] = step(cs[j])
                 for q in range(len(pan)):
                     pan[q] = step(pan[q])
-        for mats, (_, pan) in zip(state, panels):
-            lhs = jnp.where(lhs_mask, mats[0], 0.0)
+        for mats, lhs, (_, pan) in zip(state, lefts, panels):
+            q1, q2, q3 = split3(jnp.concatenate(pan, 1))
+            none = jnp.zeros((n - 6 * BLOCK, q1.shape[1]), jnp.bfloat16)
+            rhs = jnp.concatenate([q1, q2, q1, q3, q1, q2, none], 0)
+            change = lax.dot_general(lhs, rhs, NN, preferred_element_type=F32)
             for q in range(len(mats)):
-                parts = []
+                parts = [pan[q]]
                 if lo:
-                    parts.append(jnp.zeros((lo, n), F32))
-                parts.append(pan[q])
+                    parts.insert(0, mats[q][:lo] - change[:lo, q * n:(q + 1) * n])
                 if hi < n:
-                    parts.append(jnp.zeros((n - hi, n), F32))
-                full = jnp.concatenate(parts, 0)
-                mats[q] = jnp.where(inside, full, mats[q] - mm(lhs, full))
+                    parts.append(mats[q][hi:] - change[hi:, q * n:(q + 1) * n])
+                mats[q] = jnp.concatenate(parts, 0)
     return [s[1:] for s in state]
 
 
@@ -417,7 +435,10 @@
     count = sizes[0] * sizes[1] * sizes[2]
     stages = stages_of(count)
     nst = max(1, len(stages))
-    x2d = warm_start.reshape(pairs * rows, cols)
+    x2d, land_cover, prune_mask, class_resistance, source_cells, ground_cells = (
+        pltpu.with_memory_space_constraint(v, pltpu.HBM) for v in (
+            warm_start.reshape(pairs * rows, cols), land_cover, prune_mask, class_resistance,
+            source_cells.reshape(1, pairs), ground_cells.reshape(1, pairs)))
     basis = jax.ShapeDtypeStruct((3 * pairs, rows * cols), jnp.bfloat16)
     hbm = pl.BlockSpec(memory_space=pltpu.HBM)
     vm = pl.BlockSpec(memory_space=pltpu.VMEM)
@@ -448,7 +469,7 @@
             pltpu.VMEM((2, rows, cols), F32),
             pltpu.VMEM((2, rows, cols), F32),
             pltpu.VMEM((2, rows, cols), F32),
-            pltpu.VMEM((4, rows, cols), F32),
+            pltpu.VMEM((6, rows, cols), F32),
             pltpu.VMEM((2, pairs, cols), F32),
             pltpu.SemaphoreType.DMA((3, 4)),
             pltpu.SemaphoreType.DMA((3, 4)),
@@ -461,7 +482,7 @@
         compiler_params=pltpu.CompilerParams(
             collective_id=0, has_side_effects=True, vmem_limit_bytes=40 * 2**20),
         name="krylov",
-    )(land_cover, prune_mask, class_resistance, source_cells.reshape(1, pairs), ground_cells.reshape(1, pairs), x2d)
+    )(land_cover, prune_mask, class_resistance, source_cells, ground_cells, x2d)
     full = jax.ShapeDtypeStruct(warm_start.shape, F32)
     tile = 8
     return pl.pallas_call(

time: 58.2 us -> 55.9 us (0.960)
  local copies, waits for them, and re-layouts: 4.81 us -> 0 us
  Pallas kernels: 52.3 us -> 54.9 us
    unnamed x14 -> x0, local copies, waits for them, and re-layouts: 4.81 us -> none
    pallas_call x1, Pallas kernels: 37.7 us -> 39.8 us  [per_device(): pl.pallas_call(functools.partial(krylov_kernel, sizes, pieces), out_shape...]
where the time goes in v3:
time: 55.9 us; the launch traced here: 55.7 us
  Pallas kernels  54.9 us (98%)
  between operations  0.8 us (1%)
    pallas_call x1, Pallas kernels, per_device(): pl.pallas_call(functools.partial(krylov_kernel, sizes, pieces), out_shape...  39.8 us
    pallas_call x1, Pallas kernels, per_device(): pl.pallas_call(finish_kernel, out_shape=(full, full), in_specs=[vm, vm, v...  15.1 us

profile of v3, /device:TPU:0, one launch (start us, length us, event | category | flops | bytes accessed | tf_op | source)
XLA Modules:
  0.0 55.7 jit_solution(7498695839849582256)
XLA Ops:
  0.6 39.8 %krylov.1 = (bf16[384,3072]{1,0:T(8,128)(2,1)S(1)}, bf16[384,3072]{1,0:T(8,128)(2,1)S(1)}, f32[512,128]{1,0:T(8,128)S(1)}) custom-call(s32[24,128]{1,0:T(8,128)} %cover_hbm.1, s32[2,24,128]{2,1,0:T(8,128)} %prune_hbm.1, f32[16]{0:T(128)} %table_hbm.1, s32[1,128]{1,0:T(1,128)} %bitcast.5, s32[1,128]{1,0:T(1,128)} %bitcast.6, f32[3072,128]{1,0:T(8,128)} %bitcast.3), custom_call_target="tpu_custom_call" | custom-call | tf_op jit(solution)/shard_map/krylov/pallas_call | solution.py:447
  40.4 15.1 %finish.1 = (f32[128,24,128]{2,1,0:T(8,128)}, f32[128,24,128]{2,1,0:T(8,128)}) custom-call(f32[512,128]{1,0:T(8,128)S(1)} %get-tuple-element.5.gram_ref, bf16[384,3072]{1,0:T(8,128)(2,1)S(1)} %get-tuple-element.6.vh, bf16[384,3072]{1,0:T(8,128)(2,1)S(1)} %get-tuple-element.7.vl, f32[3072,128]{1,0:T(8,128)} %bitcast.4), custom_call_target="tpu_custom_call" | custom-call | tf_op jit(solution)/shard_map/finish/pallas_call | solution.py:488

commit v4 on v3

--- a/solution.py
+++ b/solution.py
@@ -130,7 +130,8 @@
         packs[0] = pack
         return carry
 
-    lax.fori_loop(0, rows // STEP, load_rows, 0)
+    last_step = rows // STEP - 1
+    lax.fori_loop(0, 2, lambda i, carry: load_rows(i * last_step, carry), 0)
     pl.semaphore_wait(barrier, expect + near)
 
     def halo(e):
@@ -170,7 +171,9 @@
     info = copies(((edge, edge_down, 0), (edge, edge_up, 1), (side, side_right, 2), (side, side_left, 3)), isend, irecv)
     start(info)
     ex = [copies(halo(e), hsend.at[e], hrecv.at[e]) for e in range(3)]
-    start(ex[0])
+    start(ex[0][:2])
+    lax.fori_loop(1, last_step, load_rows, 0)
+    start(ex[0][2:])
 
     for cp in loads[4:]:
         cp.wait()
@@ -230,7 +233,13 @@
                     packs[e + 1, hs, :] = pack
             return carry
 
-        lax.fori_loop(0, rows // STEP, body, 0)
+        last = rows // STEP - 1
+        lax.fori_loop(0, 2, lambda i, carry: body(i * last, carry), 0)
+        if e < 2:
+            start(ex[e + 1][:2])
+        lax.fori_loop(1, last, body, 0)
+        if e < 2:
+            start(ex[e + 1][2:])
 
     total_cols = cols * cells_n
     col_f = (lax.broadcasted_iota(jnp.int32, (1, cols), 1) + c * cols)
@@ -287,13 +296,11 @@
 
     wait(ex[0])
     stencil(0, first)
-    start(ex[1])
 
     gl[0][0:pairs, :] = dot3(part(0, 1), part(0, 1), NT)
     reduce_start(0, 0)
     wait(ex[1])
     stencil(1, second)
-    start(ex[2])
 
     reduce_finish(0, 0)
     gl[0][pairs:3 * pairs, :] = dot3(part(0, 2), part(1, 2), NT)
@@ -355,11 +362,12 @@
         for i in range(BLOCK):
             for cs, pan in panels:
                 f = cs[i]
-                rinv = 1.0 / f[i:i + 1, :]
+                rinv = pl.reciprocal(f[i:i + 1, :])
 
                 def step(t):
-                    top = t[i:i + 1, :] * rinv
-                    return jnp.where(sub == i, top, t - f * top)
+                    top = t[i:i + 1, :]
+                    prod = f * top
+                    return jnp.where(sub == i, top * rinv, t - prod * rinv)
 
                 for j in range(i + 1, BLOCK):
                     cs[j] = step(cs[j])

time: 55.9 us -> 56.3 us (level)
    pallas_call x1, Pallas kernels: 15.1 us -> 16.9 us  [per_device(): pl.pallas_call(finish_kernel, out_shape=(full, full), in_specs=[vm, vm, v...]
    pallas_call x1, Pallas kernels: 39.8 us -> 38.4 us  [per_device(): pl.pallas_call(functools.partial(krylov_kernel, sizes, pieces), out_shape...]
where the time goes in v4:
time: 56.3 us; the launch traced here: 56.1 us
  Pallas kernels  55.3 us (98%)
  between operations  0.8 us (1%)
    pallas_call x1, Pallas kernels, per_device(): pl.pallas_call(functools.partial(krylov_kernel, sizes, pieces), out_shape...  38.4 us
    pallas_call x1, Pallas kernels, per_device(): pl.pallas_call(finish_kernel, out_shape=(full, full), in_specs=[vm, vm, v...  16.9 us

profile of v4, /device:TPU:0, one launch (start us, length us, event | category | flops | bytes accessed | tf_op | source)
XLA Modules:
  0.0 56.1 jit_solution(14874397111186714152)
XLA Ops:
  0.6 38.4 %krylov.1 = (bf16[384,3072]{1,0:T(8,128)(2,1)S(1)}, bf16[384,3072]{1,0:T(8,128)(2,1)S(1)}, f32[512,128]{1,0:T(8,128)S(1)}) custom-call(s32[24,128]{1,0:T(8,128)} %cover_hbm.1, s32[2,24,128]{2,1,0:T(8,128)} %prune_hbm.1, f32[16]{0:T(128)} %table_hbm.1, s32[1,128]{1,0:T(1,128)} %bitcast.5, s32[1,128]{1,0:T(1,128)} %bitcast.6, f32[3072,128]{1,0:T(8,128)} %bitcast.3), custom_call_target="tpu_custom_call" | custom-call | tf_op jit(solution)/shard_map/krylov/pallas_call | solution.py:455
  39.0 16.9 %finish.1 = (f32[128,24,128]{2,1,0:T(8,128)}, f32[128,24,128]{2,1,0:T(8,128)}) custom-call(f32[512,128]{1,0:T(8,128)S(1)} %get-tuple-element.5.gram_ref, bf16[384,3072]{1,0:T(8,128)(2,1)S(1)} %get-tuple-element.6.vh, bf16[384,3072]{1,0:T(8,128)(2,1)S(1)} %get-tuple-element.7.vl, f32[3072,128]{1,0:T(8,128)} %bitcast.4), custom_call_target="tpu_custom_call" | custom-call | tf_op jit(solution)/shard_map/finish/pallas_call | solution.py:496
